TPU v7x, 256 devices: a whole 4x4x8 slice. The times are simulated.
256 devices in a mesh: lon: 32 (over z_lo, y, core), lat: 8 (over x, z_hi).
Axes of the slice: x: 4, y: 4, z: 8 (z_hi: 2, z_lo: 4; z = z_hi * 4 + z_lo), core: 2. Of those that a mesh axis runs over, the one named last changes fastest.
Arguments:
- field: float32 [2, 1536, 768, 128], P(None, 'lon', 'lat'), may hold values from -6 to 6
- lat_factor: float32 [768, 96], P('lat'), may hold values from -0.21875 to 0.21875
- lev_factor: float32 [128, 32], replicated, may hold values from -0.5 to 0.5
- old_factor: float32 [1536, 96], P('lon'), may hold values from -0.15625 to 0.15625
Outputs:
- new_factor: float32 [1536, 96], P('lon')
All inputs are finite; a program needn't handle non-finite values.
Results may differ from a plain program's by a relative error of at most 0.0003.
Values sent between devices are 32-bit elements; how exact they have to be, the bound alone decides.
A program may use at most 64 MiB of HBM per device.

v0:
```python
import jax
import jax.numpy as jnp
from jax import lax
from jax.sharding import PartitionSpec as P

HIGH = lax.Precision.HIGHEST


def body(field, lat_factor, lev_factor, old_factor):
    times, rows, lats, levs = field.shape
    levels = jnp.einsum("tijg,gs->tijs", field, lev_factor, precision=HIGH)
    partial_proj = jnp.einsum("tijs,ja->tias", levels, lat_factor, precision=HIGH)
    partial_proj = partial_proj.reshape(times, rows, -1)
    projected = lax.psum(partial_proj, "lat")
    local_weights = jnp.einsum("tik,ir->tkr", projected, old_factor, precision=HIGH)
    weights = lax.psum(local_weights, "lon")
    image = jnp.einsum("tik,tkr->ir", projected, weights, precision=HIGH)
    local_gram = jnp.dot(image.T, image, precision=HIGH)
    gram = lax.psum(local_gram, "lon")
    chol = jnp.linalg.cholesky(gram)
    solved = jax.scipy.linalg.solve_triangular(chol, image.T, lower=True)
    total_rows = rows * lax.axis_size("lon")
    return solved.T * jnp.sqrt(jnp.float32(total_rows))


def solution(mesh):
    placed = (P(None, "lon", "lat", None), P("lat", None), P(), P("lon", None))
    return jax.shard_map(
        body, mesh=mesh, in_specs=placed, out_specs=P("lon", None), check_vma=False
    )
```

profile of v0, /device:TPU:1, one launch (start us, length us, event | category | flops | bytes accessed | tf_op | source)
XLA Modules:
  0.0 619.9 jit_solution(9312035670014068513)
XLA Ops:
  6.5 0.0 copy-start
  6.5 0.0 all-reduce.3.cloned.1.call-start
  6.5 11.5 %fusion.11 = f32[2,48,96,32]{2,3,1,0:T(8,128)S(1)} fusion(f32[2,48,96,128]{3,2,1,0:T(8,128)} %param.4, f32[128,32]{0,1:T(8,128)} %param.6), kind=kOutput, calls=%fused_computation.16 | convolution fusion | flops 452984832 | bytes 5914624 | tf_op jit(solution)/shard_map/tijg,gs->tijs/dot_general | solution.py:11
  18.1 0.0 copy-done
  18.1 2.4 fusion.2
  20.5 2.9 copy.7
  23.5 4.8 reshape.13
  28.3 0.0 all-reduce.3.cloned.1.call-update
  28.3 0.0 all-reduce.5.cloned.1.call-start
  28.4 141.3 %all-reduce.3.cloned.1.call-done = f32[2,48,3072]{2,1,0:T(8,128)} async-done(((f32[2,48,3072]{2,1,0:T(8,128)}), f32[2,48,3072]{2,1,0:T(8,128)}) %all-reduce.3.cloned.1.call-update) | async-done | bytes 1179664 | tf_op jit(solution)/shard_map/psum | solution.py:14
  169.6 0.0 copy-done.2
  169.6 4.7 fusion.9
  174.4 0.0 all-reduce.5.cloned.1.call-update
  174.4 282.4 %all-reduce.5.cloned.1.call-done = f32[2,3072,96]{1,2,0:T(8,128)} async-done(((f32[2,3072,96]{1,2,0:T(8,128)}), f32[2,3072,96]{1,2,0:T(8,128)}) %all-reduce.5.cloned.1.call-update) | async-done | bytes 2359312 | tf_op jit(solution)/shard_map/psum | solution.py:16
  456.8 0.0 copy-done.1
  456.8 4.2 convolution_bitcast_fusion
  461.0 0.3 fusion.13
  461.3 133.4 %psum.23 = f32[96,96]{0,1:T(8,128)S(1)} all-reduce(f32[96,96]{0,1:T(8,128)S(1)} %fusion.13), channel_id=1, replica_groups=mesh['lon'=32,'lat'=8] {'lon'}, use_global_device_ids=true, to_apply=%region_2.0 | all-reduce | flops 9216 | bytes 73728 | tf_op jit(solution)/shard_map/psum | solution.py:19
  594.7 0.1 copy.9
  594.8 8.8 %cholesky.16 = f32[96,96]{1,0:T(8,128)S(1)} custom-call(f32[96,96]{1,0:T(8,128)S(1)} %fusion.8), custom_call_target="Cholesky" | custom-call | tf_op jit(solution)/shard_map/jit(cholesky)/cholesky | solution.py:20
  603.6 0.6 compare_reduce_fusion
  604.2 0.7 fusion.5
  604.9 7.4 %custom-call.7 = f32[1,96,96]{1,2,0:T(8,128)S(1)} custom-call(f32[1,96,96]{2,1,0:T(8,128)S(1)} %fusion.5), custom_call_target="InvertDiagBlocksLowerTriangular" | custom-call | tf_op jit(solution)/shard_map/jit(_solve_triangular)/triangular_solve | solution.py:21
  612.3 0.8 convolution_multiply_fusion
  (4 shorter events, 0.0 us)
Async XLA Ops:
  6.5 11.6 %copy-start = (f32[96,96]{1,0:T(8,128)S(1)}, f32[96,96]{1,0:T(8,128)}, u32[]{:S(2)}) copy-start(f32[96,96]{1,0:T(8,128)} %param.5) | copy-start | bytes 110596
  6.5 163.1 %all-reduce.3.cloned.1.call-start = ((), (), s32[]{:S(2)}) async-start(), calls=%async_computation | async-start | bytes 2359296 | tf_op jit(solution)/shard_map/psum | solution.py:14
  23.5 146.2 %copy-start.2 = (f32[48,96]{1,0:T(8,128)S(1)}, f32[48,96]{1,0:T(8,128)}, u32[]{:S(2)}) copy-start(f32[48,96]{1,0:T(8,128)} %param.7) | copy-start | bytes 55300
  28.3 428.4 %all-reduce.5.cloned.1.call-start = ((), (), s32[]{:S(2)}) async-start(), calls=%async_computation.1 | async-start | bytes 4718592 | tf_op jit(solution)/shard_map/psum | solution.py:16
  174.4 282.4 %copy-start.1 = (f32[2,48,3072]{2,1,0:T(8,128)S(1)}, f32[2,48,3072]{2,1,0:T(8,128)}, u32[]{:S(2)}) copy-start(f32[2,48,3072]{2,1,0:T(8,128)} %all-reduce.3.cloned.1.call-done) | copy-start | bytes 3538948
Sparse Core Ops, SparseCore 0:
  28.5 141.1 all-reduce.2
  174.5 282.2 all-reduce.4
where the time goes:
time: 625 us; the launch traced here: 620 us
  waiting for transfers between devices  424 us (68%)
  blocking collectives  133 us (21%)
  matrix products  23.9 us (4%)
  other arithmetic  17.5 us (3%)
  between operations  13.5 us (2%)
  local copies, waits for them, and re-layouts  7.86 us (1%)
    psum x1, waiting for transfers between devices, body(): weights = lax.psum(local_weights, 'lon')  282 us
    psum x1, waiting for transfers between devices, body(): projected = lax.psum(partial_proj, 'lat')  141 us
    psum x1, blocking collectives, body(): gram = lax.psum(local_gram, 'lon')  133 us
  transfers between devices with their start and end apart: 2, of which 2 were waited for; matrix products, arithmetic and copies ran while one was open for 0% of the time, Pallas kernels for 0%

commit v1 on v0

v1 whole, which is shorter than its diff:
```python
import functools

import jax
import jax.numpy as jnp
from jax import lax
from jax.experimental import pallas as pl
from jax.experimental.pallas import tpu as pltpu
from jax.sharding import PartitionSpec as P

MESH = pl.DeviceIdType.MESH
HIGHEST = lax.Precision.HIGHEST
F32, BF16 = jnp.float32, jnp.bfloat16
TIMES, ROWS, LATS, LEVS = 2, 48, 96, 128
RLAT, RLEV, RLON = 96, 32, 96
SLABS = 3
OWNERS = 12
GROUP = 32


def split(v):
    hi = v.astype(BF16)
    return hi, (v - hi.astype(F32)).astype(BF16)


def place():
    lon, lat = lax.axis_index("lon"), lax.axis_index("lat")
    return lat // 2, (lat % 2) * 4 + lon // 8, (lon // 2) % 4, lon % 2


def device(x, z, y, core):
    return (z % 4) * 8 + y * 2 + core, x * 2 + z // 4


def contract_lanes(a, b):
    return lax.dot_general(a, b, (((1,), (1,)), ((), ())), precision=HIGHEST, preferred_element_type=F32)


def gather_kernel(
    field, lat, lev, old, gram_out, image_out,
    fv, lats, lvl, proj, xr, zsrc, zr, pz, oldr, wt, wr, ws, wf, img, ir, gp, gr, gs, gf,
    fsem, xsend, xrecv, zsend, zrecv, osem, wsend, wrecv, asend, arecv, isem, gsem,
):
    x, z, y, core = place()
    slice_ = ((z + 6) % 8) // 4
    gz = (z + 6) % 4
    member = gz * 8 + y * 2 + core
    own = y * 4 + gz

    def in_group(m):
        return device(x, (2 + 4 * slice_ + m // 8) % 8, (m // 2) % 4, m % 2)

    def owner_member(o, kind):
        return (o % 4) * 8 + (o // 4) * 2 + kind

    def send(src, dst, ssem, rsem, to):
        return pltpu.make_async_remote_copy(
            src_ref=src, dst_ref=dst, send_sem=ssem, recv_sem=rsem, device_id=to, device_id_type=MESH
        )

    def arrived(ref, sem):
        pltpu.make_async_copy(ref, ref, sem).wait()

    barrier = pltpu.get_barrier_semaphore()
    for dx in (1, 2, 3):
        pl.semaphore_signal(barrier, inc=1, device_id=device((x + dx) % 4, z, y, core), device_id_type=MESH)
    for dx in range(4):
        for dz in (2, 6):
            pl.semaphore_signal(
                barrier, inc=1, device_id=device((x + dx) % 4, (z + dz) % 8, y, core), device_id_type=MESH
            )

    def greet(j, c):
        pl.semaphore_signal(barrier, inc=1, device_id=in_group((member + j) % GROUP), device_id_type=MESH)
        return c

    lax.fori_loop(1, GROUP, greet, 0)

    chunk = 16 * LATS
    loads = [
        pltpu.make_async_copy(field.at[pl.ds(k * chunk, chunk)], fv.at[pl.ds(k * chunk, chunk)], fsem.at[k])
        for k in range(6)
    ]
    for load in loads:
        load.start()

    levh, levl = split(lev[...].T)
    lev2 = jnp.concatenate(
        [jnp.concatenate([levh, levh], 1), jnp.concatenate([levl, jnp.zeros_like(levl)], 1)], 0
    )
    lats[...] = jnp.zeros_like(lats)
    lats[0:LATS, 0:RLAT] = lat[...]
    lat_pad = lats[...]
    lane = lax.broadcasted_iota(jnp.int32, (128, 128), 1)
    lat_hi, lat_lo = [], []
    for u in range(SLABS):
        tail = jnp.where(lane >= RLAT, pltpu.roll(lat_pad, 96 - 32 * u, 1), 0.0)
        hi, lo = split(jnp.concatenate([lat_pad, tail], 0))
        lat_hi.append(hi)
        lat_lo.append(lo)

    xcopies = []
    for t in range(TIMES):
        for c in range(3):
            loads[3 * t + c].wait()

            def levels(i, carry, t=t):
                f = fv[pl.ds(pl.multiple_of((t * ROWS + i) * LATS, LATS), LATS), :]
                fh, fl = split(f)
                both = jnp.concatenate([fh, fl], 1)
                both = jnp.concatenate([both, jnp.zeros((128 - LATS, 256), BF16)], 0)
                r = lax.dot_general(lev2, both, (((1,), (1,)), ((), ())), preferred_element_type=F32)
                lvl[pl.ds(i, RLEV, stride=ROWS), :] = r[:RLEV] + r[RLEV:]
                return carry

            lax.fori_loop(16 * c, 16 * c + 16, levels, 0, unroll=4)
        for u in range(SLABS):
            parts = [
                jnp.concatenate([lvl[pl.ds((4 * d + v) * ROWS, ROWS), :] for d in range(8)], 0) for v in (u, 3)
            ]
            hi, lo = split(jnp.concatenate(parts, 1))
            r = (
                jnp.dot(hi, lat_hi[u], preferred_element_type=F32)
                + jnp.dot(lo, lat_hi[u], preferred_element_type=F32)
                + jnp.dot(hi, lat_lo[u], preferred_element_type=F32)
            )
            for d in range(8):
                proj[t, d, u] = r[d * ROWS : (d + 1) * ROWS]
        if t == 0:
            pl.semaphore_wait(barrier, 3 + 8 + GROUP - 1)
            oldcopy = send(old, oldr, osem.at[0], osem.at[1], device(x, (z + 2) % 8, y, core))
            oldcopy.start()
        row = []
        for dx in (1, 2, 3):
            to = (x + dx) % 4
            copy = send(
                proj.at[t, pl.ds(2 * to, 2)], xr.at[t, dx - 1], xsend.at[t, dx - 1], xrecv.at[t, dx - 1],
                device(to, z, y, core),
            )
            copy.start()
            row.append(copy)
        xcopies.append(row)

    up = z // 4
    zcopies = []
    for t in range(TIMES):
        for copy in xcopies[t]:
            copy.wait_recv()
        total = proj[t, pl.ds(2 * x, 2)] + xr[t, 0] + xr[t, 1] + xr[t, 2]
        zsrc[t] = total
        row = [
            send(zsrc.at[t, up], zr.at[t, 0], zsend.at[t, 0], zrecv.at[t, 0], device(x, (z + 2) % 8, y, core)),
            send(zsrc.at[t, 1 - up], zr.at[t, 1], zsend.at[t, 1], zrecv.at[t, 1], device(x, (z + 6) % 8, y, core)),
        ]
        for copy in row:
            copy.start()
        zcopies.append(row)

    def reduce_start(src, slots, kind, ssem, rsem):
        mine = jnp.logical_and(core == kind, y < 3)

        def one(j, c):
            o = (own + j) % OWNERS
            m = owner_member(o, kind)
            part = src.at[:, pl.ds(pl.multiple_of(8 * o, 8), 8), :]

            @pl.when(m != member)
            def _():
                send(part, slots.at[member], ssem, rsem, in_group(m)).start()

            @pl.when(m == member)
            def _():
                pltpu.make_async_copy(part, slots.at[member], rsem).start()

            return c

        lax.fori_loop(0, OWNERS, one, 0)
        return mine

    def reduce_finish(slots, summed, full, mine, rsem, ssem2, rsem2):
        @pl.when(mine)
        def _():
            arrived(slots, rsem)
            acc = slots[0]
            for k in range(1, GROUP):
                acc = acc + slots[k]
            summed[...] = acc
            here = full.at[:, pl.ds(pl.multiple_of(8 * own, 8), 8), :]
            pltpu.make_async_copy(summed, here, rsem2).start()

            def one(j, c):
                send(summed, here, ssem2, rsem2, in_group((member + j) % GROUP)).start()
                return c

            lax.fori_loop(1, GROUP, one, 0)

    def drain(src, slots, mine, ssem, ssem2):
        @pl.when(mine)
        def _():
            arrived(src.at[:, pl.ds(0, 88), :], ssem)
            arrived(slots.at[pl.ds(0, GROUP - 1)], ssem2)

        @pl.when(jnp.logical_not(mine))
        def _():
            arrived(src, ssem)

    oldcopy.wait_recv()
    old_t = oldr[...].T
    mines = []
    for t in range(TIMES):
        for copy in zcopies[t]:
            copy.wait_recv()
        pz[t] = zr[t, 0] + zr[t, 1]
        for u in range(SLABS):
            wt[t, u] = jnp.dot(old_t, pz[t, u], precision=HIGHEST, preferred_element_type=F32)
        mines.append(reduce_start(wt.at[t], wr.at[t], t, wsend.at[t], wrecv.at[t]))
    for t in range(TIMES):
        reduce_finish(wr.at[t], ws.at[t], wf.at[t], mines[t], wrecv.at[t], asend.at[t], arecv.at[t])
    acc = jnp.zeros((ROWS, RLON), F32)
    for t in range(TIMES):
        arrived(wf.at[t], arecv.at[t])
        for u in range(SLABS):
            acc = acc + contract_lanes(pz[t, u], wf[t, u])
    img[:, 0:RLON] = acc
    img[:, RLON:] = jnp.zeros((ROWS, 128 - RLON), F32)

    for dx in range(4):
        for k, dz in enumerate((2, 6)):
            send(
                img, ir.at[2 * dx + k], isem.at[0], isem.at[1], device((x + dx) % 4, (z + dz) % 8, y, core)
            ).start()
    arrived(ir, isem.at[1])
    image = ir[0]
    for k in range(1, 8):
        image = image + ir[k]
    image_out[...] = image
    gp[0] = lax.dot_general(
        image, image, (((0,), (0,)), ((), ())), precision=HIGHEST, preferred_element_type=F32
    )[0:RLON]
    mine = reduce_start(gp, gr, 0, gsem.at[0], gsem.at[1])
    reduce_finish(gr, gs, gf, mine, gsem.at[1], gsem.at[2], gsem.at[3])
    arrived(gf, gsem.at[3])
    gram_out[...] = gf[0]

    oldcopy.wait_send()
    for row in xcopies + zcopies:
        for copy in row:
            copy.wait_send()
    for t in range(TIMES):
        drain(wt.at[t], wr.at[t], mines[t], wsend.at[t], asend.at[t])
    drain(gp, gr, mine, gsem.at[0], gsem.at[2])
    arrived(ir, isem.at[0])


BLOCK = 8


def solve_kernel(total_rows, gram, image, out, uref):
    image_t = image[...].T[0:RLON]
    right = jnp.concatenate([image_t, jnp.zeros((RLON, 128 - ROWS), F32)], 1)
    uref[...] = jnp.zeros_like(uref)
    sub = lax.broadcasted_iota(jnp.int32, (BLOCK, 256), 0)
    for j in range(RLON // BLOCK):
        at = BLOCK * j
        panel = jnp.concatenate([gram[at : at + BLOCK, :], right[at : at + BLOCK, :]], 1)
        if j:
            above = uref[0:at, :]
            panel = panel - lax.dot_general(
                above[:, at : at + BLOCK], above, (((0,), (0,)), ((), ())), precision=HIGHEST,
                preferred_element_type=F32,
            )
        col = [jnp.broadcast_to(panel[:, at + q : at + q + 1], (BLOCK, 128)) for q in range(BLOCK)]
        d = [[None] * BLOCK for _ in range(BLOCK)]
        for q in range(BLOCK):
            for p in range(q + 1):
                d[q][p] = jnp.broadcast_to(col[p][q : q + 1, :], (BLOCK, 128))
        inv = []
        for p in range(BLOCK):
            inv.append(lax.rsqrt(d[p][p]))
            for q in range(p + 1, BLOCK):
                d[q][p] = d[q][p] * inv[p]
            for q in range(p + 1, BLOCK):
                for r in range(p + 1, q + 1):
                    d[q][r] = d[q][r] - d[q][p] * d[r][p]
        wide = lambda v: jnp.concatenate([v, v], 1)
        rows = []
        for p in range(BLOCK):
            v = jnp.broadcast_to(panel[p : p + 1, :], (BLOCK, 256))
            for q in range(p):
                v = v - wide(d[p][q]) * rows[q]
            rows.append(v * wide(inv[p]))
        block = rows[0]
        for p in range(1, BLOCK):
            block = jnp.where(sub == p, rows[p], block)
        uref[at : at + BLOCK, :] = block
    y = uref[:, 128:256].T
    out[...] = y[0:ROWS, :] * jnp.sqrt(F32(total_rows))


def body(field, lat_factor, lev_factor, old_factor):
    vmem = pl.BlockSpec(memory_space=pltpu.VMEM)
    dma = pltpu.SemaphoreType.DMA
    field = field.reshape(TIMES * ROWS * LATS, LEVS)
    total_rows = ROWS * lax.axis_size("lon")
    gram, image = pl.pallas_call(
        gather_kernel,
        out_shape=(jax.ShapeDtypeStruct((RLON, 128), F32), jax.ShapeDtypeStruct((ROWS, 128), F32)),
        in_specs=[pl.BlockSpec(memory_space=pl.ANY), vmem, vmem, vmem],
        out_specs=(vmem, vmem),
        scratch_shapes=[
            pltpu.VMEM((TIMES * ROWS * LATS, LEVS), F32),
            pltpu.VMEM((128, 128), F32),
            pltpu.VMEM((RLEV * ROWS, 128), F32),
            pltpu.VMEM((TIMES, 8, SLABS, ROWS, 128), F32),
            pltpu.VMEM((TIMES, 3, 2, SLABS, ROWS, 128), F32),
            pltpu.VMEM((TIMES, 2, SLABS, ROWS, 128), F32),
            pltpu.VMEM((TIMES, 2, SLABS, ROWS, 128), F32),
            pltpu.VMEM((TIMES, SLABS, ROWS, 128), F32),
            pltpu.VMEM((ROWS, RLON), F32),
            pltpu.VMEM((TIMES, SLABS, RLON, 128), F32),
            pltpu.VMEM((TIMES, GROUP, SLABS, 8, 128), F32),
            pltpu.VMEM((TIMES, SLABS, 8, 128), F32),
            pltpu.VMEM((TIMES, SLABS, RLON, 128), F32),
            pltpu.VMEM((ROWS, 128), F32),
            pltpu.VMEM((8, ROWS, 128), F32),
            pltpu.VMEM((1, RLON, 128), F32),
            pltpu.VMEM((GROUP, 1, 8, 128), F32),
            pltpu.VMEM((1, 8, 128), F32),
            pltpu.VMEM((1, RLON, 128), F32),
            dma((6,)),
            dma((TIMES, 3)),
            dma((TIMES, 3)),
            dma((TIMES, 2)),
            dma((TIMES, 2)),
            dma((2,)),
            dma((TIMES,)),
            dma((TIMES,)),
            dma((TIMES,)),
            dma((TIMES,)),
            dma((2,)),
            dma((4,)),
        ],
        compiler_params=pltpu.CompilerParams(
            collective_id=0, has_side_effects=True, vmem_limit_bytes=32 * 1024 * 1024
        ),
    )(field, lat_factor, lev_factor, old_factor)
    return pl.pallas_call(
        functools.partial(solve_kernel, total_rows),
        out_shape=jax.ShapeDtypeStruct((ROWS, RLON), F32),
        in_specs=[vmem, vmem],
        out_specs=vmem,
        scratch_shapes=[pltpu.VMEM((RLON, 256), F32)],
    )(gram, image)


def solution(mesh):
    placed = (P(None, "lon", "lat", None), P("lat", None), P(), P("lon", None))
    return jax.shard_map(
        body, mesh=mesh, in_specs=placed, out_specs=P("lon", None), check_vma=False
    )
```

time: 625 us -> 83.1 us (0.13)
  waiting for transfers between devices: 424 us -> 0 us
  blocking collectives: 133 us -> 0 us
  Pallas kernels: 0 us -> 76.8 us
  matrix products: 23.9 us -> 0 us
  other arithmetic: 17.5 us -> 0 us
  between operations: 13.5 us -> 0.03 us
    psum x2 -> x0, waiting for transfers between devices: 424 us -> none  [the longest x1 282 us: body(): weights = lax.psum(local_weights, 'lon')]
    psum x1 -> x0, blocking collectives: 133 us -> none  [body(): gram = lax.psum(local_gram, 'lon')]
    pallas_call x0 -> x2, Pallas kernels: none -> 76.8 us  [the longest x1 70 us: body(): pl.pallas_call(gather_kernel, out_shape=(jax.ShapeDtypeStruct((RLON, 128)...]
    dot_general x5 -> x0, matrix products: 23.1 us -> none  [the longest x1 11.5 us: body(): levels = jnp.einsum('tijg,gs->tijs', field, lev_factor, precision=HIGH)]
    another operation x5 -> x0, other arithmetic: 17.5 us -> none  [the longest x3 9.45 us: body(): chol = jnp.linalg.cholesky(gram)]
  transfers between devices with their start and end apart: 2 -> 0, of which waited for: 2 -> 0; matrix products, arithmetic and copies ran while one was open for 0% -> 0% of each run, Pallas kernels for 0% -> 0%
where the time goes in v1:
time: 83.1 us; the launch traced here: 82.8 us
  Pallas kernels  76.8 us (92%)
  local copies, waits for them, and re-layouts  5.89 us (7%)
    pallas_call x1, Pallas kernels, body(): pl.pallas_call(gather_kernel, out_shape=(jax.ShapeDtypeStruct((RLON, 128)...  70 us
    pallas_call x1, Pallas kernels, body(): pl.pallas_call(functools.partial(solve_kernel, total_rows), out_shape=jax...  6.83 us
    unnamed x11, local copies, waits for them, and re-layouts  5.89 us

profile of v1, /device:TPU:1, one launch (start us, length us, event | category | flops | bytes accessed | tf_op | source)
XLA Modules:
  0.0 82.8 jit_solution(8074455211346327866)
XLA Ops:
  0.0 0.8 copy.5.lev
  0.8 0.0 copy-start
  0.8 2.3 %copy-done = f32[2,48,96,128]{3,2,1,0:T(8,128)S(1)} copy-done((f32[2,48,96,128]{3,2,1,0:T(8,128)S(1)}, f32[2,48,96,128]{3,2,1,0:T(8,128)}, u32[]{:S(2)}) %copy-start) | copy-done | bytes 4718616
  3.2 0.0 copy-start.1
  3.2 0.8 copy-done.1
  4.0 0.0 copy-start.3
  4.0 0.7 copy-done.3
  4.7 70.0 %shard_map.46 = (f32[96,128]{1,0:T(8,128)S(1)}, f32[48,128]{1,0:T(8,128)S(1)}) custom-call(f32[9216,128]{1,0:T(8,128)S(1)} %bitcast.1, f32[96,96]{1,0:T(8,128)S(1)} %copy-done.1, f32[128,32]{1,0:T(8,128)S(1)} %copy.5.lev, f32[48,96]{1,0:T(8,128)S(1)} %copy-done.3), custom_call_target="tpu_custom_call" | custom-call | tf_op jit(solution)/shard_map/pallas_call | solution.py:304
  74.7 0.0 copy-start.2
  74.7 0.6 copy-done.2
  75.3 0.0 copy-start.4
  75.3 0.6 copy-done.4
  75.9 6.8 %shard_map.47 = f32[48,96]{1,0:T(8,128)} custom-call(f32[96,128]{1,0:T(8,128)} %copy-done.2, f32[48,128]{1,0:T(8,128)} %copy-done.4), custom_call_target="tpu_custom_call" | custom-call | tf_op jit(solution)/shard_map/pallas_call | solution.py:346
Async XLA Ops:
  0.8 2.3 %copy-start = (f32[2,48,96,128]{3,2,1,0:T(8,128)S(1)}, f32[2,48,96,128]{3,2,1,0:T(8,128)}, u32[]{:S(2)}) copy-start(f32[2,48,96,128]{3,2,1,0:T(8,128)} %param.4) | copy-start | bytes 14155780
  3.2 0.8 copy-start.1
  4.0 0.7 copy-start.3
  74.7 0.6 copy-start.2
  75.3 0.6 copy-start.4

commit v2 on v0

v2 whole, which is shorter than its diff:
```python
import functools

import jax
import jax.numpy as jnp
from jax import lax
from jax.experimental import pallas as pl
from jax.experimental.pallas import tpu as pltpu
from jax.sharding import PartitionSpec as P

MESH = pl.DeviceIdType.MESH
HIGHEST = lax.Precision.HIGHEST
F32, BF16 = jnp.float32, jnp.bfloat16
TIMES, ROWS, LATS, LEVS = 2, 48, 96, 128
RLAT, RLEV, RLON = 96, 32, 96
SLABS = 3
BLOCKS = TIMES * SLABS
PART = 2 * RLON // 8
SCHEDULE = sorted((b + lag, kind, b) for b in range(BLOCKS) for kind, lag in enumerate((0, 2.6, 6.2, 8.8)))


def split(v):
    hi = v.astype(BF16)
    return hi, (v - hi.astype(F32)).astype(BF16)


def place():
    lon, lat = lax.axis_index("lon"), lax.axis_index("lat")
    return lat // 2, (lat % 2) * 4 + lon // 8, (lon // 2) % 4, lon % 2


def device(x, z, y, core):
    return (z % 4) * 8 + y * 2 + core, x * 2 + z // 4


def contract_lanes(a, b):
    return lax.dot_general(a, b, (((1,), (1,)), ((), ())), precision=HIGHEST, preferred_element_type=F32)


BLOCK = 8


def solve(total_rows, gram, image, out, uref):
    image_t = image[...].T[0:RLON]
    right = jnp.concatenate([image_t, jnp.zeros((RLON, 128 - ROWS), F32)], 1)
    uref[...] = jnp.zeros_like(uref)
    sub = lax.broadcasted_iota(jnp.int32, (BLOCK, 256), 0)
    for j in range(RLON // BLOCK):
        at = BLOCK * j
        panel = jnp.concatenate([gram[at : at + BLOCK, :], right[at : at + BLOCK, :]], 1)
        if j:
            above = uref[0:at, :]
            panel = panel - lax.dot_general(
                above[:, at : at + BLOCK], above, (((0,), (0,)), ((), ())), precision=HIGHEST,
                preferred_element_type=F32,
            )
        col = [jnp.broadcast_to(panel[:, at + q : at + q + 1], (BLOCK, 128)) for q in range(BLOCK)]
        d = [[None] * BLOCK for _ in range(BLOCK)]
        for q in range(BLOCK):
            for p in range(q + 1):
                d[q][p] = jnp.broadcast_to(col[p][q : q + 1, :], (BLOCK, 128))
        inv = []
        for p in range(BLOCK):
            inv.append(lax.rsqrt(d[p][p]))
            for q in range(p + 1, BLOCK):
                d[q][p] = d[q][p] * inv[p]
            for q in range(p + 1, BLOCK):
                for r in range(p + 1, q + 1):
                    d[q][r] = d[q][r] - d[q][p] * d[r][p]
        wide = lambda v: jnp.concatenate([v, v], 1)
        rows = []
        for p in range(BLOCK):
            v = jnp.broadcast_to(panel[p : p + 1, :], (BLOCK, 256))
            for q in range(p):
                v = v - wide(d[p][q]) * rows[q]
            rows.append(v * wide(inv[p]))
        block = rows[0]
        for p in range(1, BLOCK):
            block = jnp.where(sub == p, rows[p], block)
        uref[at : at + BLOCK, :] = block
    y = uref[:, 128:256].T
    out[...] = y[0:ROWS, :] * jnp.sqrt(F32(total_rows))


def hooi_kernel(
    total_rows, field, lat, lev_t, old, out,
    fv, lat_in, lev_in, old_in, lats, lvl, proj, xr, pz, wt, wr, ws, wz, wf, img, ir, summed, home, gp, gr, gh, go, gf,
    uref, fsem, csem, xsem, rsem, zsem, asem, isem, hsem, gsem,
):
    x, z, y, core = place()
    me = y * 2 + core

    def send(src, dst, sems, to):
        copy = pltpu.make_async_remote_copy(
            src_ref=src, dst_ref=dst, send_sem=sems.at[0], recv_sem=sems.at[1], device_id=to, device_id_type=MESH
        )
        copy.start()
        return copy

    def arrived(ref, sem):
        pltpu.make_async_copy(ref, ref, sem).wait()

    chunk = 16 * LATS
    loads = [
        pltpu.make_async_copy(field.at[pl.ds(k * chunk, chunk)], fv.at[pl.ds(k * chunk, chunk)], fsem.at[k])
        for k in range(6)
    ]
    small = [
        pltpu.make_async_copy(src, dst, csem.at[k])
        for k, (src, dst) in enumerate(((lev_t, lev_in), (lat, lat_in), (old, old_in)))
    ]
    for load in small + loads:
        load.start()

    x_peers = [device((x + dx) % 4, z, y, core) for dx in (1, 2, 3)]
    z_peers = [device(x, (z + dz) % 8, y, core) for dz in range(1, 8)]
    yc_peers = [device(x, z, ((me + j) % 8) // 2, (me + j) % 2) for j in range(1, 8)]
    i_peers = [device((x + dx) % 4, (z + dz) % 8, y, core) for dx in range(4) for dz in (2, 6)]
    g_steps = [(dy, dz) for dy in range(4) for dz in (0, 1, 7, 2 if dy < 2 else 6)][1:]
    g_peers = [device(x, (z + dz) % 8, (y + dy) % 4, core) for dy, dz in g_steps]
    also = [device(x, (z + 2) % 8, (y + 2) % 4, core)]
    greeted = x_peers + z_peers + yc_peers + i_peers[2:] + [
        peer for (dy, dz), peer in zip(g_steps, g_peers) if dy and dz
    ] + also
    barrier = pltpu.get_barrier_semaphore()
    for peer in greeted:
        pl.semaphore_signal(barrier, inc=1, device_id=peer, device_id_type=MESH)

    small[0].wait()
    small[1].wait()
    levh, levl = split(lev_in[...])
    lev2 = jnp.concatenate(
        [jnp.concatenate([levh, levh], 1), jnp.concatenate([levl, jnp.zeros_like(levl)], 1)], 0
    )
    lats[...] = jnp.zeros_like(lats)
    lats[0:LATS, 0:RLAT] = lat_in[...]
    lat_pad = lats[...]
    lane = lax.broadcasted_iota(jnp.int32, (128, 128), 1)
    lat_hi, lat_lo = [], []
    for u in range(SLABS):
        tail = jnp.where(lane >= RLAT, pltpu.roll(lat_pad, 96 - 32 * u, 1), 0.0)
        hi, lo = split(jnp.concatenate([lat_pad, tail], 0))
        lat_hi.append(hi)
        lat_lo.append(lo)

    xcopies = []
    for t in range(TIMES):
        for c in range(3):
            loads[3 * t + c].wait()

            def levels(i, carry, t=t):
                f = fv[pl.ds(pl.multiple_of((t * ROWS + i) * LATS, LATS), LATS), :]
                fh, fl = split(f)
                both = jnp.concatenate([fh, fl], 1)
                both = jnp.concatenate([both, jnp.zeros((128 - LATS, 256), BF16)], 0)
                r = lax.dot_general(lev2, both, (((1,), (1,)), ((), ())), preferred_element_type=F32)
                lvl[pl.ds(i, RLEV, stride=ROWS), :] = r[:RLEV] + r[RLEV:]
                return carry

            lax.fori_loop(16 * c, 16 * c + 16, levels, 0, unroll=4)
        for u in range(SLABS):
            parts = [
                jnp.concatenate([lvl[pl.ds((4 * d + v) * ROWS, ROWS), :] for d in range(8)], 0) for v in (u, 3)
            ]
            hi, lo = split(jnp.concatenate(parts, 1))
            r = (
                jnp.dot(hi, lat_hi[u], preferred_element_type=F32)
                + jnp.dot(lo, lat_hi[u], preferred_element_type=F32)
                + jnp.dot(hi, lat_lo[u], preferred_element_type=F32)
            )
            b = t * SLABS + u
            for d in range(8):
                proj[b, d // 2, d % 2] = r[d * ROWS : (d + 1) * ROWS]
            if b == 0:
                pl.semaphore_wait(barrier, len(greeted))
            xcopies.append(
                [send(proj.at[b, (x + k + 1) % 4], xr.at[b, k], xsem.at[b, k], x_peers[k]) for k in range(3)]
            )

    small[2].wait()
    old_t = old_in[...].T
    acc = jnp.zeros((ROWS, RLON), F32)

    for at, kind, b in SCHEDULE:
        if kind == 0:
            for copy in xcopies[b]:
                copy.wait_recv()
            pz[b] = proj[b, x] + xr[b, 0] + xr[b, 1] + xr[b, 2]
            for s in range(2):
                wt[b, s * RLON : (s + 1) * RLON] = jnp.dot(
                    old_t, pz[b, s], precision=HIGHEST, preferred_element_type=F32
                )
            for k in range(7):
                part = wt.at[b, pl.ds(pl.multiple_of(PART * ((me + k + 1) % 8), 8), PART)]
                send(part, wr.at[b, k], rsem.at[b], yc_peers[k])
        elif kind == 1:
            arrived(wr.at[b], rsem.at[b, 1])
            part = wt[b, pl.ds(pl.multiple_of(PART * me, 8), PART)]
            for k in range(7):
                part = part + wr[b, k]
            ws[b, 0] = part
            for k in range(7):
                send(ws.at[b, 0], wz.at[b, k], zsem.at[b], z_peers[k])
        elif kind == 2:
            arrived(wz.at[b], zsem.at[b, 1])
            part = ws[b, 0]
            for k in range(7):
                part = part + wz[b, k]
            mine = pl.ds(pl.multiple_of(PART * me, 8), PART)
            wf[b, mine] = part
            for k in range(7):
                send(wf.at[b, mine], wf.at[b, mine], asem.at[b], yc_peers[k])
        else:
            arrived(wr.at[b], asem.at[b, 1])
            for s in range(2):
                acc = acc + contract_lanes(pz[b, s], wf[b, s * RLON : (s + 1) * RLON])
    img[:, 0:RLON] = acc
    img[:, RLON:] = jnp.zeros((ROWS, 128 - RLON), F32)
    for k in range(8):
        send(img, ir.at[k], isem, i_peers[k])
    arrived(ir, isem.at[1])
    image = ir[0]
    for k in range(1, 8):
        image = image + ir[k]
    summed[...] = image
    back = send(summed, home, hsem, z_peers[1])
    gp[...] = lax.dot_general(
        image, image, (((0,), (0,)), ((), ())), precision=HIGHEST, preferred_element_type=F32
    )[0:RLON]
    half = RLON // 2
    sibling = device(x, z, y, 1 - core)
    mine, other = (pl.ds(pl.multiple_of(half * c, 8), half) for c in (core, 1 - core))
    first = send(gp.at[other], gr, gsem.at[0], sibling)
    first.wait_recv()
    gh[...] = gp[mine] + gr[...]
    for k in range(15):
        send(gh, go.at[k], gsem.at[1], g_peers[k])
    arrived(go, gsem.at[1, 1])
    total = gh[...]
    for k in range(15):
        total = total + go[k]
    gf[mine] = total
    last = send(gf.at[mine], gf.at[mine], gsem.at[2], sibling)
    last.wait_recv()
    back.wait_recv()
    solve(total_rows, gf, home, out, uref)

    for row in xcopies:
        for copy in row:
            copy.wait_send()
    for b in range(BLOCKS):
        arrived(wr.at[b], rsem.at[b, 0])
        arrived(wz.at[b], zsem.at[b, 0])
        arrived(wr.at[b], asem.at[b, 0])
    arrived(ir, isem.at[0])
    back.wait_send()
    first.wait_send()
    arrived(go, gsem.at[1, 0])
    last.wait_send()


def body(field, lat_factor, lev_factor, old_factor):
    vmem = pl.BlockSpec(memory_space=pltpu.VMEM)
    dma = pltpu.SemaphoreType.DMA
    field = field.reshape(TIMES * ROWS * LATS, LEVS)
    total_rows = ROWS * lax.axis_size("lon")
    return pl.pallas_call(
        functools.partial(hooi_kernel, total_rows),
        out_shape=jax.ShapeDtypeStruct((ROWS, RLON), F32),
        in_specs=[pl.BlockSpec(memory_space=pltpu.HBM)] * 4,
        out_specs=vmem,
        scratch_shapes=[
            pltpu.VMEM((TIMES * ROWS * LATS, LEVS), F32),
            pltpu.VMEM((LATS, RLAT), F32),
            pltpu.VMEM((RLEV, LEVS), F32),
            pltpu.VMEM((ROWS, RLON), F32),
            pltpu.VMEM((128, 128), F32),
            pltpu.VMEM((RLEV * ROWS, 128), F32),
            pltpu.VMEM((BLOCKS, 4, 2, ROWS, 128), F32),
            pltpu.VMEM((BLOCKS, 3, 2, ROWS, 128), F32),
            pltpu.VMEM((BLOCKS, 2, ROWS, 128), F32),
            pltpu.VMEM((BLOCKS, 2 * RLON, 128), F32),
            pltpu.VMEM((BLOCKS, 7, PART, 128), F32),
            pltpu.VMEM((BLOCKS, 1, PART, 128), F32),
            pltpu.VMEM((BLOCKS, 7, PART, 128), F32),
            pltpu.VMEM((BLOCKS, 2 * RLON, 128), F32),
            pltpu.VMEM((ROWS, 128), F32),
            pltpu.VMEM((8, ROWS, 128), F32),
            pltpu.VMEM((ROWS, 128), F32),
            pltpu.VMEM((ROWS, 128), F32),
            pltpu.VMEM((RLON, 128), F32),
            pltpu.VMEM((RLON // 2, 128), F32),
            pltpu.VMEM((RLON // 2, 128), F32),
            pltpu.VMEM((15, RLON // 2, 128), F32),
            pltpu.VMEM((RLON, 128), F32),
            pltpu.VMEM((RLON, 256), F32),
            dma((6,)),
            dma((3,)),
            dma((BLOCKS, 3, 2)),
            dma((BLOCKS, 2)),
            dma((BLOCKS, 2)),
            dma((BLOCKS, 2)),
            dma((2,)),
            dma((2,)),
            dma((3, 2)),
        ],
        compiler_params=pltpu.CompilerParams(
            collective_id=0, has_side_effects=True, vmem_limit_bytes=56 * 1024 * 1024
        ),
    )(field, lat_factor, lev_factor.T, old_factor)


def solution(mesh):
    placed = (P(None, "lon", "lat", None), P("lat", None), P(), P("lon", None))
    return jax.shard_map(
        body, mesh=mesh, in_specs=placed, out_specs=P("lon", None), check_vma=False
    )
```

time: 625 us -> 67.9 us (0.11)
  waiting for transfers between devices: 424 us -> 0 us
  blocking collectives: 133 us -> 0 us
  Pallas kernels: 0 us -> 66.4 us
  matrix products: 23.9 us -> 0 us
  other arithmetic: 17.5 us -> 0 us
  between operations: 13.5 us -> 0.01 us
  local copies, waits for them, and re-layouts: 7.86 us -> 1.35 us
    psum x2 -> x0, waiting for transfers between devices: 424 us -> none  [the longest x1 282 us: body(): weights = lax.psum(local_weights, 'lon')]
    psum x1 -> x0, blocking collectives: 133 us -> none  [body(): gram = lax.psum(local_gram, 'lon')]
    pallas_call x0 -> x1, Pallas kernels: none -> 66.4 us  [body(): pl.pallas_call(functools.partial(hooi_kernel, total_rows), out_shape=jax....]
    dot_general x5 -> x0, matrix products: 23.1 us -> none  [the longest x1 11.5 us: body(): levels = jnp.einsum('tijg,gs->tijs', field, lev_factor, precision=HIGH)]
    another operation x5 -> x0, other arithmetic: 17.5 us -> none  [the longest x3 9.45 us: body(): chol = jnp.linalg.cholesky(gram)]
  transfers between devices with their start and end apart: 2 -> 0, of which waited for: 2 -> 0; matrix products, arithmetic and copies ran while one was open for 0% -> 0% of each run, Pallas kernels for 0% -> 0%
where the time goes in v2:
time: 67.9 us; the launch traced here: 67.8 us
  Pallas kernels  66.4 us (98%)
  local copies, waits for them, and re-layouts  1.35 us (2%)
    pallas_call x1, Pallas kernels, body(): pl.pallas_call(functools.partial(hooi_kernel, total_rows), out_shape=jax....  66.4 us

profile of v2, /device:TPU:1, one launch (start us, length us, event | category | flops | bytes accessed | tf_op | source)
XLA Modules:
  0.0 67.8 jit_solution(9264305765980632967)
XLA Ops:
  0.0 66.4 %shard_map.46 = f32[48,96]{1,0:T(8,128)} custom-call(f32[9216,128]{1,0:T(8,128)} %bitcast.2, f32[96,96]{1,0:T(8,128)} %lat.1, f32[32,128]{1,0:T(8,128)} %bitcast.3, f32[48,96]{1,0:T(8,128)} %old.1), custom_call_target="tpu_custom_call" | custom-call | tf_op jit(solution)/shard_map/pallas_call | solution.py:266
  66.4 1.3 %copy.6 = f32[48,96]{1,0:T(8,128)} copy(f32[48,96]{1,0:T(8,128)} %shard_map.46) | data formatting | bytes 36864

commit v3 on v2

--- a/solution.py
+++ b/solution.py
@@ -36,55 +36,58 @@
     return lax.dot_general(a, b, (((1,), (1,)), ((), ())), precision=HIGHEST, preferred_element_type=F32)
 
 
-BLOCK = 8
-
-
-def solve(total_rows, gram, image, out, uref):
-    image_t = image[...].T[0:RLON]
-    right = jnp.concatenate([image_t, jnp.zeros((RLON, 128 - ROWS), F32)], 1)
-    uref[...] = jnp.zeros_like(uref)
-    sub = lax.broadcasted_iota(jnp.int32, (BLOCK, 256), 0)
-    for j in range(RLON // BLOCK):
-        at = BLOCK * j
-        panel = jnp.concatenate([gram[at : at + BLOCK, :], right[at : at + BLOCK, :]], 1)
-        if j:
-            above = uref[0:at, :]
-            panel = panel - lax.dot_general(
-                above[:, at : at + BLOCK], above, (((0,), (0,)), ((), ())), precision=HIGHEST,
-                preferred_element_type=F32,
-            )
-        col = [jnp.broadcast_to(panel[:, at + q : at + q + 1], (BLOCK, 128)) for q in range(BLOCK)]
-        d = [[None] * BLOCK for _ in range(BLOCK)]
-        for q in range(BLOCK):
-            for p in range(q + 1):
-                d[q][p] = jnp.broadcast_to(col[p][q : q + 1, :], (BLOCK, 128))
-        inv = []
-        for p in range(BLOCK):
-            inv.append(lax.rsqrt(d[p][p]))
-            for q in range(p + 1, BLOCK):
-                d[q][p] = d[q][p] * inv[p]
-            for q in range(p + 1, BLOCK):
+PANEL = 16
+
+
+def solve(total_rows, top, image_t, out, yt):
+    tiles = RLON // 8
+    left = [top[8 * r : 8 * r + 8] for r in range(tiles)]
+    right = [image_t[8 * r : 8 * r + 8] for r in range(tiles)]
+    sub = lax.broadcasted_iota(jnp.int32, (8, 128), 0)
+    diagonal = lax.broadcasted_iota(jnp.int32, (8, 128), 1) - sub
+    spread = lambda v: jnp.broadcast_to(v, (8, 128))
+    for j in range(RLON // PANEL):
+        at, first = PANEL * j, PANEL // 8 * j
+        col = [
+            [spread(left[first + s][:, at + q : at + q + 1]) if q >= 8 * s else None for q in range(PANEL)]
+            for s in range(PANEL // 8)
+        ]
+        d = [[spread(col[p // 8][q][p % 8 : p % 8 + 1]) for p in range(q + 1)] for q in range(PANEL)]
+        vl = [spread(left[first + p // 8][p % 8 : p % 8 + 1]) for p in range(PANEL)]
+        vr = [spread(right[first + p // 8][p % 8 : p % 8 + 1]) for p in range(PANEL)]
+        for p in range(PANEL):
+            inv = lax.rsqrt(d[p][p])
+            for q in range(p + 1, PANEL):
+                d[q][p] = d[q][p] * inv
+            for q in range(p + 1, PANEL):
                 for r in range(p + 1, q + 1):
                     d[q][r] = d[q][r] - d[q][p] * d[r][p]
-        wide = lambda v: jnp.concatenate([v, v], 1)
-        rows = []
-        for p in range(BLOCK):
-            v = jnp.broadcast_to(panel[p : p + 1, :], (BLOCK, 256))
-            for q in range(p):
-                v = v - wide(d[p][q]) * rows[q]
-            rows.append(v * wide(inv[p]))
-        block = rows[0]
-        for p in range(1, BLOCK):
-            block = jnp.where(sub == p, rows[p], block)
-        uref[at : at + BLOCK, :] = block
-    y = uref[:, 128:256].T
-    out[...] = y[0:ROWS, :] * jnp.sqrt(F32(total_rows))
+            vl[p], vr[p] = vl[p] * inv, vr[p] * inv
+            for q in range(p + 1, PANEL):
+                vl[q] = vl[q] - d[q][p] * vl[p]
+                vr[q] = vr[q] - d[q][p] * vr[p]
+        for s in range(PANEL // 8):
+            rows = vr[8 * s]
+            for p in range(1, 8):
+                rows = jnp.where(sub == p, vr[8 * s + p], rows)
+            yt[at + 8 * s : at + 8 * s + 8] = rows
+        for r in range(first + PANEL // 8, tiles):
+            ml, mr = [], []
+            for p in range(PANEL):
+                c = jnp.sum(jnp.where(diagonal == 8 * r, vl[p], 0.0), axis=1, keepdims=True)
+                ml.append(c * vl[p])
+                mr.append(c * vr[p])
+            while len(ml) > 1:
+                ml = [a + b for a, b in zip(ml[::2], ml[1::2])]
+                mr = [a + b for a, b in zip(mr[::2], mr[1::2])]
+            left[r], right[r] = left[r] - ml[0], right[r] - mr[0]
+    out[...] = yt[...].T[0:ROWS] * jnp.sqrt(F32(total_rows))
 
 
 def hooi_kernel(
     total_rows, field, lat, lev_t, old, out,
     fv, lat_in, lev_in, old_in, lats, lvl, proj, xr, pz, wt, wr, ws, wz, wf, img, ir, summed, home, gp, gr, gh, go, gf,
-    uref, fsem, csem, xsem, rsem, zsem, asem, isem, hsem, gsem,
+    yt, fsem, csem, xsem, rsem, zsem, asem, isem, hsem, gsem,
 ):
     x, z, y, core = place()
     me = y * 2 + core
@@ -242,7 +245,8 @@
     last = send(gf.at[mine], gf.at[mine], gsem.at[2], sibling)
     last.wait_recv()
     back.wait_recv()
-    solve(total_rows, gf, home, out, uref)
+    image_t = jnp.concatenate([home[...].T[0:RLON], jnp.zeros((RLON, 128 - ROWS), F32)], 1)
+    solve(total_rows, gf[...], image_t, out, yt)
 
     for row in xcopies:
         for copy in row:
@@ -265,7 +269,7 @@
     total_rows = ROWS * lax.axis_size("lon")
     return pl.pallas_call(
         functools.partial(hooi_kernel, total_rows),
-        out_shape=jax.ShapeDtypeStruct((ROWS, RLON), F32),
+        out_shape=pltpu.VMEM((ROWS, RLON), F32),
         in_specs=[pl.BlockSpec(memory_space=pltpu.HBM)] * 4,
         out_specs=vmem,
         scratch_shapes=[
@@ -292,7 +296,7 @@
             pltpu.VMEM((RLON // 2, 128), F32),
             pltpu.VMEM((15, RLON // 2, 128), F32),
             pltpu.VMEM((RLON, 128), F32),
-            pltpu.VMEM((RLON, 256), F32),
+            pltpu.VMEM((RLON, 128), F32),
             dma((6,)),
             dma((3,)),
             dma((BLOCKS, 3, 2)),
@@ -304,9 +308,9 @@
             dma((3, 2)),
         ],
         compiler_params=pltpu.CompilerParams(
-            collective_id=0, has_side_effects=True, vmem_limit_bytes=56 * 1024 * 1024
+            collective_id=0, has_side_effects=True, vmem_limit_bytes=48 * 1024 * 1024
         ),
-    )(field, lat_factor, lev_factor.T, old_factor)
+    )(*(pltpu.with_memory_space_constraint(v, pltpu.HBM) for v in (field, lat_factor, lev_factor.T, old_factor)))
 
 
 def solution(mesh):

time: 67.9 us -> 64.1 us (0.944)
  Pallas kernels: 66.4 us -> 63.4 us
  local copies, waits for them, and re-layouts: 1.35 us -> 0.61 us
    pallas_call x1, Pallas kernels: 66.4 us -> 63.4 us  [body(): pl.pallas_call(functools.partial(hooi_kernel, total_rows), out_shape=pltp...]
    unnamed x1, local copies, waits for them, and re-layouts: 1.35 us -> 0.61 us
where the time goes in v3:
time: 64.1 us; the launch traced here: 64 us
  Pallas kernels  63.4 us (99%)
    pallas_call x1, Pallas kernels, body(): pl.pallas_call(functools.partial(hooi_kernel, total_rows), out_shape=pltp...  63.4 us

profile of v3, /device:TPU:1, one launch (start us, length us, event | category | flops | bytes accessed | tf_op | source)
XLA Modules:
  0.0 64.0 jit_solution(16517283652075939869)
XLA Ops:
  0.0 63.4 %shard_map.46 = f32[48,96]{1,0:T(8,128)S(1)} custom-call(f32[9216,128]{1,0:T(8,128)} %bitcast.2, f32[96,96]{1,0:T(8,128)} %lat.1, f32[32,128]{1,0:T(8,128)} %bitcast.3, f32[48,96]{1,0:T(8,128)} %old.1), custom_call_target="tpu_custom_call" | custom-call | tf_op jit(solution)/shard_map/pallas_call | solution.py:270
  63.4 0.6 copy.6

commit v4 on v3

--- a/solution.py
+++ b/solution.py
@@ -14,6 +14,7 @@
 RLAT, RLEV, RLON = 96, 32, 96
 SLABS = 3
 BLOCKS = TIMES * SLABS
+CHUNK = 16
 PART = 2 * RLON // 8
 SCHEDULE = sorted((b + lag, kind, b) for b in range(BLOCKS) for kind, lag in enumerate((0, 2.6, 6.2, 8.8)))
 
@@ -34,6 +35,43 @@
 
 def contract_lanes(a, b):
     return lax.dot_general(a, b, (((1,), (1,)), ((), ())), precision=HIGHEST, preferred_element_type=F32)
+
+
+IMAGE_ROWS = 40
+
+
+def lanes_of(v):
+    return lax.broadcasted_iota(jnp.int32, v.shape, 1)
+
+
+def pack_image(v):
+    last = v[IMAGE_ROWS:]
+    tail = [pltpu.roll(last, 96 - 32 * k, 1) for k in range(3)]
+    tail = jnp.concatenate(tail + [jnp.zeros((IMAGE_ROWS - 24, 128), F32)], 0)
+    return jnp.where(lanes_of(tail) < RLON, v[:IMAGE_ROWS], tail)
+
+
+def unpack_image(v):
+    last = jnp.zeros((8, 128), F32)
+    for k in range(3):
+        piece = pltpu.roll(v[8 * k : 8 * k + 8], 32 + 32 * k, 1)
+        last = jnp.where(lanes_of(last) // 32 == k, piece, last)
+    return jnp.concatenate([jnp.where(lanes_of(v) < RLON, v, 0.0), last], 0)
+
+
+def pack_gram(g):
+    half = RLON // 2
+    top, low = g[:half], g[half:RLON]
+    lane, row = lanes_of(top), lax.broadcasted_iota(jnp.int32, top.shape, 0)
+    rest = jnp.where(lane <= half, pltpu.roll(top, 1, 1), pltpu.roll(top, 16, 1))
+    return jnp.where(lane <= row, pltpu.roll(low, 128 - half, 1), rest)
+
+
+def unpack_gram(v):
+    half = RLON // 2
+    top = jnp.where(lanes_of(v) < half, pltpu.roll(v, 127, 1), pltpu.roll(v, 112, 1))
+    square = jnp.concatenate([v, jnp.zeros((128 - half, 128), F32)], 0).T
+    return jnp.concatenate([top, pltpu.roll(square[:half], half, 1)], 0)
 
 
 PANEL = 16
@@ -102,7 +140,7 @@
     def arrived(ref, sem):
         pltpu.make_async_copy(ref, ref, sem).wait()
 
-    chunk = 16 * LATS
+    chunk = CHUNK * LATS
     loads = [
         pltpu.make_async_copy(field.at[pl.ds(k * chunk, chunk)], fv.at[pl.ds(k * chunk, chunk)], fsem.at[k])
         for k in range(6)
@@ -121,9 +159,8 @@
     g_steps = [(dy, dz) for dy in range(4) for dz in (0, 1, 7, 2 if dy < 2 else 6)][1:]
     g_peers = [device(x, (z + dz) % 8, (y + dy) % 4, core) for dy, dz in g_steps]
     also = [device(x, (z + 2) % 8, (y + 2) % 4, core)]
-    greeted = x_peers + z_peers + yc_peers + i_peers[2:] + [
-        peer for (dy, dz), peer in zip(g_steps, g_peers) if dy and dz
-    ] + also
+    far = [peer for (dy, dz), peer in zip(g_steps, g_peers) if dy and dz] + also
+    greeted = far + i_peers[2:] + z_peers + yc_peers + x_peers
     barrier = pltpu.get_barrier_semaphore()
     for peer in greeted:
         pl.semaphore_signal(barrier, inc=1, device_id=peer, device_id_type=MESH)
@@ -145,34 +182,39 @@
         lat_hi.append(hi)
         lat_lo.append(lo)
 
+    def levels(t, c):
+        def one(i, carry):
+            f = fv[pl.ds(pl.multiple_of((t * ROWS + i) * LATS, LATS), LATS), :]
+            fh, fl = split(f)
+            both = jnp.concatenate([fh, fl], 1)
+            both = jnp.concatenate([both, jnp.zeros((128 - LATS, 256), BF16)], 0)
+            r = lax.dot_general(lev2, both, (((1,), (1,)), ((), ())), preferred_element_type=F32)
+            lvl[pl.ds(i, RLEV, stride=ROWS), :] = r[:RLEV] + r[RLEV:]
+            return carry
+
+        loads[3 * t + c].wait()
+        lax.fori_loop(CHUNK * c, CHUNK * c + CHUNK, one, 0, unroll=4)
+
+    def latitudes(t, u):
+        parts = [
+            jnp.concatenate([lvl[pl.ds((4 * d + v) * ROWS, ROWS), :] for d in range(8)], 0) for v in (u, 3)
+        ]
+        hi, lo = split(jnp.concatenate(parts, 1))
+        r = (
+            jnp.dot(hi, lat_hi[u], preferred_element_type=F32)
+            + jnp.dot(lo, lat_hi[u], preferred_element_type=F32)
+            + jnp.dot(hi, lat_lo[u], preferred_element_type=F32)
+        )
+        for d in range(8):
+            proj[t * SLABS + u, d // 2, d % 2] = r[d * ROWS : (d + 1) * ROWS]
+
     xcopies = []
     for t in range(TIMES):
         for c in range(3):
-            loads[3 * t + c].wait()
-
-            def levels(i, carry, t=t):
-                f = fv[pl.ds(pl.multiple_of((t * ROWS + i) * LATS, LATS), LATS), :]
-                fh, fl = split(f)
-                both = jnp.concatenate([fh, fl], 1)
-                both = jnp.concatenate([both, jnp.zeros((128 - LATS, 256), BF16)], 0)
-                r = lax.dot_general(lev2, both, (((1,), (1,)), ((), ())), preferred_element_type=F32)
-                lvl[pl.ds(i, RLEV, stride=ROWS), :] = r[:RLEV] + r[RLEV:]
-                return carry
-
-            lax.fori_loop(16 * c, 16 * c + 16, levels, 0, unroll=4)
+            levels(t, c)
         for u in range(SLABS):
-            parts = [
-                jnp.concatenate([lvl[pl.ds((4 * d + v) * ROWS, ROWS), :] for d in range(8)], 0) for v in (u, 3)
-            ]
-            hi, lo = split(jnp.concatenate(parts, 1))
-            r = (
-                jnp.dot(hi, lat_hi[u], preferred_element_type=F32)
-                + jnp.dot(lo, lat_hi[u], preferred_element_type=F32)
-                + jnp.dot(hi, lat_lo[u], preferred_element_type=F32)
-            )
+            latitudes(t, u)
             b = t * SLABS + u
-            for d in range(8):
-                proj[b, d // 2, d % 2] = r[d * ROWS : (d + 1) * ROWS]
             if b == 0:
                 pl.semaphore_wait(barrier, len(greeted))
             xcopies.append(
@@ -200,12 +242,12 @@
             part = wt[b, pl.ds(pl.multiple_of(PART * me, 8), PART)]
             for k in range(7):
                 part = part + wr[b, k]
-            ws[b, 0] = part
-            for k in range(7):
-                send(ws.at[b, 0], wz.at[b, k], zsem.at[b], z_peers[k])
+            ws[b] = part
+            for k in range(7):
+                send(ws.at[b], wz.at[b, k], zsem.at[b], z_peers[k])
         elif kind == 2:
             arrived(wz.at[b], zsem.at[b, 1])
-            part = ws[b, 0]
+            part = ws[b]
             for k in range(7):
                 part = part + wz[b, k]
             mine = pl.ds(pl.multiple_of(PART * me, 8), PART)
@@ -216,20 +258,20 @@
             arrived(wr.at[b], asem.at[b, 1])
             for s in range(2):
                 acc = acc + contract_lanes(pz[b, s], wf[b, s * RLON : (s + 1) * RLON])
-    img[:, 0:RLON] = acc
-    img[:, RLON:] = jnp.zeros((ROWS, 128 - RLON), F32)
+    img[...] = pack_image(jnp.concatenate([acc, jnp.zeros((ROWS, 128 - RLON), F32)], 1))
     for k in range(8):
         send(img, ir.at[k], isem, i_peers[k])
     arrived(ir, isem.at[1])
     image = ir[0]
     for k in range(1, 8):
         image = image + ir[k]
+    image = unpack_image(image)
     summed[...] = image
     back = send(summed, home, hsem, z_peers[1])
-    gp[...] = lax.dot_general(
-        image, image, (((0,), (0,)), ((), ())), precision=HIGHEST, preferred_element_type=F32
-    )[0:RLON]
-    half = RLON // 2
+    gp[...] = pack_gram(
+        lax.dot_general(image, image, (((0,), (0,)), ((), ())), precision=HIGHEST, preferred_element_type=F32)
+    )
+    half = RLON // 4
     sibling = device(x, z, y, 1 - core)
     mine, other = (pl.ds(pl.multiple_of(half * c, 8), half) for c in (core, 1 - core))
     first = send(gp.at[other], gr, gsem.at[0], sibling)
@@ -246,7 +288,7 @@
     last.wait_recv()
     back.wait_recv()
     image_t = jnp.concatenate([home[...].T[0:RLON], jnp.zeros((RLON, 128 - ROWS), F32)], 1)
-    solve(total_rows, gf[...], image_t, out, yt)
+    solve(total_rows, unpack_gram(gf[...]), image_t, out, yt)
 
     for row in xcopies:
         for copy in row:
@@ -284,18 +326,18 @@
             pltpu.VMEM((BLOCKS, 2, ROWS, 128), F32),
             pltpu.VMEM((BLOCKS, 2 * RLON, 128), F32),
             pltpu.VMEM((BLOCKS, 7, PART, 128), F32),
-            pltpu.VMEM((BLOCKS, 1, PART, 128), F32),
+            pltpu.VMEM((BLOCKS, PART, 128), F32),
             pltpu.VMEM((BLOCKS, 7, PART, 128), F32),
             pltpu.VMEM((BLOCKS, 2 * RLON, 128), F32),
-            pltpu.VMEM((ROWS, 128), F32),
-            pltpu.VMEM((8, ROWS, 128), F32),
+            pltpu.VMEM((IMAGE_ROWS, 128), F32),
+            pltpu.VMEM((8, IMAGE_ROWS, 128), F32),
             pltpu.VMEM((ROWS, 128), F32),
             pltpu.VMEM((ROWS, 128), F32),
-            pltpu.VMEM((RLON, 128), F32),
             pltpu.VMEM((RLON // 2, 128), F32),
+            pltpu.VMEM((RLON // 4, 128), F32),
+            pltpu.VMEM((RLON // 4, 128), F32),
+            pltpu.VMEM((15, RLON // 4, 128), F32),
             pltpu.VMEM((RLON // 2, 128), F32),
-            pltpu.VMEM((15, RLON // 2, 128), F32),
-            pltpu.VMEM((RLON, 128), F32),
             pltpu.VMEM((RLON, 128), F32),
             dma((6,)),
             dma((3,)),

time: 64.1 us -> 62.3 us (0.972)
  Pallas kernels: 63.4 us -> 61.6 us
    pallas_call x1, Pallas kernels: 63.4 us -> 61.6 us  [body(): pl.pallas_call(functools.partial(hooi_kernel, total_rows), out_shape=pltp...]
where the time goes in v4:
time: 62.3 us; the launch traced here: 62.2 us
  Pallas kernels  61.6 us (99%)
    pallas_call x1, Pallas kernels, body(): pl.pallas_call(functools.partial(hooi_kernel, total_rows), out_shape=pltp...  61.6 us

profile of v4, /device:TPU:1, one launch (start us, length us, event | category | flops | bytes accessed | tf_op | source)
XLA Modules:
  0.0 62.2 jit_solution(6952255186446623819)
XLA Ops:
  0.0 61.6 %shard_map.46 = f32[48,96]{1,0:T(8,128)S(1)} custom-call(f32[9216,128]{1,0:T(8,128)} %bitcast.2, f32[96,96]{1,0:T(8,128)} %lat.1, f32[32,128]{1,0:T(8,128)} %bitcast.3, f32[48,96]{1,0:T(8,128)} %old.1), custom_call_target="tpu_custom_call" | custom-call | tf_op jit(solution)/shard_map/pallas_call | solution.py:312
  61.6 0.6 copy.6

commit v5 on v4

--- a/solution.py
+++ b/solution.py
@@ -13,10 +13,9 @@
 TIMES, ROWS, LATS, LEVS = 2, 48, 96, 128
 RLAT, RLEV, RLON = 96, 32, 96
 SLABS = 3
-BLOCKS = TIMES * SLABS
-CHUNK = 16
-PART = 2 * RLON // 8
-SCHEDULE = sorted((b + lag, kind, b) for b in range(BLOCKS) for kind, lag in enumerate((0, 2.6, 6.2, 8.8)))
+BLOCKS = TIMES * SLABS * 2
+PART = RLON // 8
+SCHEDULE = sorted((b + lag, kind, b) for b in range(BLOCKS) for kind, lag in enumerate((0, 4.6, 11, 16)))
 
 
 def split(v):
@@ -125,14 +124,14 @@
 def hooi_kernel(
     total_rows, field, lat, lev_t, old, out,
     fv, lat_in, lev_in, old_in, lats, lvl, proj, xr, pz, wt, wr, ws, wz, wf, img, ir, summed, home, gp, gr, gh, go, gf,
-    yt, fsem, csem, xsem, rsem, zsem, asem, isem, hsem, gsem,
+    yt, fsem, csem, sent, xsem, rsem, zsem, asem, isem, hsem, gsem,
 ):
     x, z, y, core = place()
     me = y * 2 + core
 
-    def send(src, dst, sems, to):
+    def send(src, dst, sent, landed, to):
         copy = pltpu.make_async_remote_copy(
-            src_ref=src, dst_ref=dst, send_sem=sems.at[0], recv_sem=sems.at[1], device_id=to, device_id_type=MESH
+            src_ref=src, dst_ref=dst, send_sem=sent, recv_sem=landed, device_id=to, device_id_type=MESH
         )
         copy.start()
         return copy
@@ -140,10 +139,10 @@
     def arrived(ref, sem):
         pltpu.make_async_copy(ref, ref, sem).wait()
 
-    chunk = CHUNK * LATS
+    chunk = ROWS * LATS
     loads = [
         pltpu.make_async_copy(field.at[pl.ds(k * chunk, chunk)], fv.at[pl.ds(k * chunk, chunk)], fsem.at[k])
-        for k in range(6)
+        for k in range(TIMES)
     ]
     small = [
         pltpu.make_async_copy(src, dst, csem.at[k])
@@ -182,7 +181,7 @@
         lat_hi.append(hi)
         lat_lo.append(lo)
 
-    def levels(t, c):
+    def levels(t):
         def one(i, carry):
             f = fv[pl.ds(pl.multiple_of((t * ROWS + i) * LATS, LATS), LATS), :]
             fh, fl = split(f)
@@ -192,8 +191,8 @@
             lvl[pl.ds(i, RLEV, stride=ROWS), :] = r[:RLEV] + r[RLEV:]
             return carry
 
-        loads[3 * t + c].wait()
-        lax.fori_loop(CHUNK * c, CHUNK * c + CHUNK, one, 0, unroll=4)
+        loads[t].wait()
+        lax.fori_loop(0, ROWS, one, 0, unroll=16)
 
     def latitudes(t, u):
         parts = [
@@ -206,101 +205,94 @@
             + jnp.dot(hi, lat_lo[u], preferred_element_type=F32)
         )
         for d in range(8):
-            proj[t * SLABS + u, d // 2, d % 2] = r[d * ROWS : (d + 1) * ROWS]
-
-    xcopies = []
+            proj[2 * (t * SLABS + u) + d % 2, d // 2] = r[d * ROWS : (d + 1) * ROWS]
+
     for t in range(TIMES):
-        for c in range(3):
-            levels(t, c)
+        levels(t)
         for u in range(SLABS):
             latitudes(t, u)
-            b = t * SLABS + u
-            if b == 0:
+            if t + u == 0:
                 pl.semaphore_wait(barrier, len(greeted))
-            xcopies.append(
-                [send(proj.at[b, (x + k + 1) % 4], xr.at[b, k], xsem.at[b, k], x_peers[k]) for k in range(3)]
-            )
+            for b in range(2 * (t * SLABS + u), 2 * (t * SLABS + u) + 2):
+                for k in range(3):
+                    send(proj.at[b, (x + k + 1) % 4], xr.at[b, k], sent.at[0], xsem.at[b], x_peers[k])
 
     small[2].wait()
-    old_t = old_in[...].T
-    acc = jnp.zeros((ROWS, RLON), F32)
+    place_of = lambda r: 16 * (r // PART) + r % PART
+    to_slots = (
+        place_of(lax.broadcasted_iota(jnp.int32, (128, 128), 0)) == lax.broadcasted_iota(jnp.int32, (128, 128), 1)
+    ).astype(F32)
+    to_slots = jnp.where(lax.broadcasted_iota(jnp.int32, (128, 128), 0) < RLON, to_slots, 0.0)
+    old_t = jnp.dot(old_in[...], to_slots[:RLON], precision=HIGHEST, preferred_element_type=F32).T
+    wf[...] = jnp.zeros_like(wf)
+    acc = jnp.zeros((ROWS, 128), F32)
 
     for at, kind, b in SCHEDULE:
         if kind == 0:
-            for copy in xcopies[b]:
-                copy.wait_recv()
+            arrived(xr.at[b], xsem.at[b])
             pz[b] = proj[b, x] + xr[b, 0] + xr[b, 1] + xr[b, 2]
-            for s in range(2):
-                wt[b, s * RLON : (s + 1) * RLON] = jnp.dot(
-                    old_t, pz[b, s], precision=HIGHEST, preferred_element_type=F32
-                )
-            for k in range(7):
-                part = wt.at[b, pl.ds(pl.multiple_of(PART * ((me + k + 1) % 8), 8), PART)]
-                send(part, wr.at[b, k], rsem.at[b], yc_peers[k])
+            part = jnp.dot(old_t, pz[b], precision=HIGHEST, preferred_element_type=F32)
+            for k in range(8):
+                wt[b, k] = part[16 * k : 16 * k + PART]
+            for k in range(7):
+                send(wt.at[b, (me + k + 1) % 8], wr.at[b, k], sent.at[1], rsem.at[b], yc_peers[k])
         elif kind == 1:
-            arrived(wr.at[b], rsem.at[b, 1])
-            part = wt[b, pl.ds(pl.multiple_of(PART * me, 8), PART)]
+            arrived(wr.at[b], rsem.at[b])
+            part = wt[b, me]
             for k in range(7):
                 part = part + wr[b, k]
             ws[b] = part
             for k in range(7):
-                send(ws.at[b], wz.at[b, k], zsem.at[b], z_peers[k])
+                send(ws.at[b], wz.at[b, k], sent.at[2], zsem.at[b], z_peers[k])
         elif kind == 2:
-            arrived(wz.at[b], zsem.at[b, 1])
+            arrived(wz.at[b], zsem.at[b])
             part = ws[b]
             for k in range(7):
                 part = part + wz[b, k]
-            mine = pl.ds(pl.multiple_of(PART * me, 8), PART)
-            wf[b, mine] = part
-            for k in range(7):
-                send(wf.at[b, mine], wf.at[b, mine], asem.at[b], yc_peers[k])
+            wf[b, me, 0:PART] = part
+            mine = wf.at[b, me, pl.ds(0, PART)]
+            for k in range(7):
+                send(mine, mine, sent.at[3], asem.at[b], yc_peers[k])
         else:
-            arrived(wr.at[b], asem.at[b, 1])
-            for s in range(2):
-                acc = acc + contract_lanes(pz[b, s], wf[b, s * RLON : (s + 1) * RLON])
-    img[...] = pack_image(jnp.concatenate([acc, jnp.zeros((ROWS, 128 - RLON), F32)], 1))
+            arrived(wr.at[b], asem.at[b])
+            acc = acc + contract_lanes(pz[b], wf[b].reshape(128, 128))
+    img[...] = pack_image(contract_lanes(acc, to_slots))
     for k in range(8):
-        send(img, ir.at[k], isem, i_peers[k])
-    arrived(ir, isem.at[1])
+        send(img, ir.at[k], sent.at[4], isem, i_peers[k])
+    arrived(ir, isem)
     image = ir[0]
     for k in range(1, 8):
         image = image + ir[k]
     image = unpack_image(image)
     summed[...] = image
-    back = send(summed, home, hsem, z_peers[1])
+    back = send(summed, home, sent.at[5], hsem, z_peers[1])
     gp[...] = pack_gram(
         lax.dot_general(image, image, (((0,), (0,)), ((), ())), precision=HIGHEST, preferred_element_type=F32)
     )
     half = RLON // 4
     sibling = device(x, z, y, 1 - core)
     mine, other = (pl.ds(pl.multiple_of(half * c, 8), half) for c in (core, 1 - core))
-    first = send(gp.at[other], gr, gsem.at[0], sibling)
+    first = send(gp.at[other], gr, sent.at[6], gsem.at[0], sibling)
     first.wait_recv()
     gh[...] = gp[mine] + gr[...]
     for k in range(15):
-        send(gh, go.at[k], gsem.at[1], g_peers[k])
-    arrived(go, gsem.at[1, 1])
+        send(gh, go.at[k], sent.at[7], gsem.at[1], g_peers[k])
+    arrived(go, gsem.at[1])
     total = gh[...]
     for k in range(15):
         total = total + go[k]
     gf[mine] = total
-    last = send(gf.at[mine], gf.at[mine], gsem.at[2], sibling)
+    last = send(gf.at[mine], gf.at[mine], sent.at[8], gsem.at[2], sibling)
     last.wait_recv()
     back.wait_recv()
     image_t = jnp.concatenate([home[...].T[0:RLON], jnp.zeros((RLON, 128 - ROWS), F32)], 1)
     solve(total_rows, unpack_gram(gf[...]), image_t, out, yt)
 
-    for row in xcopies:
-        for copy in row:
-            copy.wait_send()
-    for b in range(BLOCKS):
-        arrived(wr.at[b], rsem.at[b, 0])
-        arrived(wz.at[b], zsem.at[b, 0])
-        arrived(wr.at[b], asem.at[b, 0])
-    arrived(ir, isem.at[0])
+    for k, ref in enumerate((xr, wr, wz, wr, ir)):
+        arrived(ref, sent.at[k])
     back.wait_send()
     first.wait_send()
-    arrived(go, gsem.at[1, 0])
+    arrived(go, sent.at[7])
     last.wait_send()
 
 
@@ -321,14 +313,14 @@
             pltpu.VMEM((ROWS, RLON), F32),
             pltpu.VMEM((128, 128), F32),
             pltpu.VMEM((RLEV * ROWS, 128), F32),
-            pltpu.VMEM((BLOCKS, 4, 2, ROWS, 128), F32),
-            pltpu.VMEM((BLOCKS, 3, 2, ROWS, 128), F32),
-            pltpu.VMEM((BLOCKS, 2, ROWS, 128), F32),
-            pltpu.VMEM((BLOCKS, 2 * RLON, 128), F32),
+            pltpu.VMEM((BLOCKS, 4, ROWS, 128), F32),
+            pltpu.VMEM((BLOCKS, 3, ROWS, 128), F32),
+            pltpu.VMEM((BLOCKS, ROWS, 128), F32),
+            pltpu.VMEM((BLOCKS, 8, PART, 128), F32),
             pltpu.VMEM((BLOCKS, 7, PART, 128), F32),
             pltpu.VMEM((BLOCKS, PART, 128), F32),
             pltpu.VMEM((BLOCKS, 7, PART, 128), F32),
-            pltpu.VMEM((BLOCKS, 2 * RLON, 128), F32),
+            pltpu.VMEM((BLOCKS, 8, 16, 128), F32),
             pltpu.VMEM((IMAGE_ROWS, 128), F32),
             pltpu.VMEM((8, IMAGE_ROWS, 128), F32),
             pltpu.VMEM((ROWS, 128), F32),
@@ -339,15 +331,16 @@
             pltpu.VMEM((15, RLON // 4, 128), F32),
             pltpu.VMEM((RLON // 2, 128), F32),
             pltpu.VMEM((RLON, 128), F32),
-            dma((6,)),
+            dma((TIMES,)),
             dma((3,)),
-            dma((BLOCKS, 3, 2)),
-            dma((BLOCKS, 2)),
-            dma((BLOCKS, 2)),
-            dma((BLOCKS, 2)),
-            dma((2,)),
-            dma((2,)),
-            dma((3, 2)),
+            dma((9,)),
+            dma((BLOCKS,)),
+            dma((BLOCKS,)),
+            dma((BLOCKS,)),
+            dma((BLOCKS,)),
+            dma,
+            dma,
+            dma((3,)),
         ],
         compiler_params=pltpu.CompilerParams(
             collective_id=0, has_side_effects=True, vmem_limit_bytes=48 * 1024 * 1024

time: 62.3 us -> 59.9 us (0.961)
  Pallas kernels: 61.6 us -> 59.1 us
    pallas_call x1, Pallas kernels: 61.6 us -> 59.1 us  [body(): pl.pallas_call(functools.partial(hooi_kernel, total_rows), out_shape=pltp...]
where the time goes in v5:
time: 59.9 us; the launch traced here: 59.8 us
  Pallas kernels  59.1 us (99%)
  local copies, waits for them, and re-layouts  0.61 us (1%)
    pallas_call x1, Pallas kernels, body(): pl.pallas_call(functools.partial(hooi_kernel, total_rows), out_shape=pltp...  59.1 us

profile of v5, /device:TPU:1, one launch (start us, length us, event | category | flops | bytes accessed | tf_op | source)
XLA Modules:
  0.0 59.8 jit_solution(3757982940369305600)
XLA Ops:
  0.0 59.1 %shard_map.46 = f32[48,96]{1,0:T(8,128)S(1)} custom-call(f32[9216,128]{1,0:T(8,128)} %bitcast.2, f32[96,96]{1,0:T(8,128)} %lat.1, f32[32,128]{1,0:T(8,128)} %bitcast.3, f32[48,96]{1,0:T(8,128)} %old.1), custom_call_target="tpu_custom_call" | custom-call | tf_op jit(solution)/shard_map/pallas_call | solution.py:304
  59.2 0.6 %copy.6 = f32[48,96]{1,0:T(8,128)} copy(f32[48,96]{1,0:T(8,128)S(1)} %shard_map.46) | data formatting | bytes 36864

commit v6 on v5

--- a/solution.py
+++ b/solution.py
@@ -1,4 +1,5 @@
 import functools
+import math
 
 import jax
 import jax.numpy as jnp
@@ -14,6 +15,7 @@
 RLAT, RLEV, RLON = 96, 32, 96
 SLABS = 3
 BLOCKS = TIMES * SLABS * 2
+LOADS = (0, 16), (16, 32), (48, 48)
 PART = RLON // 8
 SCHEDULE = sorted((b + lag, kind, b) for b in range(BLOCKS) for kind, lag in enumerate((0, 4.6, 11, 16)))
 
@@ -124,7 +126,7 @@
 def hooi_kernel(
     total_rows, field, lat, lev_t, old, out,
     fv, lat_in, lev_in, old_in, lats, lvl, proj, xr, pz, wt, wr, ws, wz, wf, img, ir, summed, home, gp, gr, gh, go, gf,
-    yt, fsem, csem, sent, xsem, rsem, zsem, asem, isem, hsem, gsem,
+    yt, fsem, csem, passed, sent, xsem, rsem, zsem, asem, isem, hsem, gsem,
 ):
     x, z, y, core = place()
     me = y * 2 + core
@@ -139,10 +141,11 @@
     def arrived(ref, sem):
         pltpu.make_async_copy(ref, ref, sem).wait()
 
-    chunk = ROWS * LATS
     loads = [
-        pltpu.make_async_copy(field.at[pl.ds(k * chunk, chunk)], fv.at[pl.ds(k * chunk, chunk)], fsem.at[k])
-        for k in range(TIMES)
+        pltpu.make_async_copy(
+            field.at[pl.ds(at * LATS, rows * LATS)], fv.at[pl.ds(at * LATS, rows * LATS)], fsem.at[k]
+        )
+        for k, (at, rows) in enumerate(LOADS)
     ]
     small = [
         pltpu.make_async_copy(src, dst, csem.at[k])
@@ -152,17 +155,18 @@
         load.start()
 
     x_peers = [device((x + dx) % 4, z, y, core) for dx in (1, 2, 3)]
+    y_peers = [device(x, z, (y + dy) % 4, core) for dy in (1, 2, 3)]
     z_peers = [device(x, (z + dz) % 8, y, core) for dz in range(1, 8)]
     yc_peers = [device(x, z, ((me + j) % 8) // 2, (me + j) % 2) for j in range(1, 8)]
     i_peers = [device((x + dx) % 4, (z + dz) % 8, y, core) for dx in range(4) for dz in (2, 6)]
     g_steps = [(dy, dz) for dy in range(4) for dz in (0, 1, 7, 2 if dy < 2 else 6)][1:]
     g_peers = [device(x, (z + dz) % 8, (y + dy) % 4, core) for dy, dz in g_steps]
-    also = [device(x, (z + 2) % 8, (y + 2) % 4, core)]
-    far = [peer for (dy, dz), peer in zip(g_steps, g_peers) if dy and dz] + also
-    greeted = far + i_peers[2:] + z_peers + yc_peers + x_peers
+
+    greeted = x_peers + yc_peers + [z_peers[k] for k in (1, 5, 0, 6)]
     barrier = pltpu.get_barrier_semaphore()
     for peer in greeted:
         pl.semaphore_signal(barrier, inc=1, device_id=peer, device_id_type=MESH)
+    told = x_peers + y_peers + [z_peers[1], z_peers[5]]
 
     small[0].wait()
     small[1].wait()
@@ -181,18 +185,19 @@
         lat_hi.append(hi)
         lat_lo.append(lo)
 
-    def levels(t):
+    def levels(k):
         def one(i, carry):
-            f = fv[pl.ds(pl.multiple_of((t * ROWS + i) * LATS, LATS), LATS), :]
+            f = fv[pl.ds(pl.multiple_of(i * LATS, LATS), LATS), :]
             fh, fl = split(f)
             both = jnp.concatenate([fh, fl], 1)
             both = jnp.concatenate([both, jnp.zeros((128 - LATS, 256), BF16)], 0)
             r = lax.dot_general(lev2, both, (((1,), (1,)), ((), ())), preferred_element_type=F32)
-            lvl[pl.ds(i, RLEV, stride=ROWS), :] = r[:RLEV] + r[RLEV:]
+            lvl[pl.ds(lax.rem(i, ROWS), RLEV, stride=ROWS), :] = r[:RLEV] + r[RLEV:]
             return carry
 
-        loads[t].wait()
-        lax.fori_loop(0, ROWS, one, 0, unroll=16)
+        loads[k].wait()
+        at, rows = LOADS[k]
+        lax.fori_loop(at, at + rows, one, 0, unroll=16)
 
     def latitudes(t, u):
         parts = [
@@ -208,15 +213,19 @@
             proj[2 * (t * SLABS + u) + d % 2, d // 2] = r[d * ROWS : (d + 1) * ROWS]
 
     for t in range(TIMES):
-        levels(t)
+        for k in ((0, 1), (2,))[t]:
+            levels(k)
         for u in range(SLABS):
             latitudes(t, u)
             if t + u == 0:
                 pl.semaphore_wait(barrier, len(greeted))
+                for peer in told:
+                    pl.semaphore_signal(passed, inc=1, device_id=peer, device_id_type=MESH)
             for b in range(2 * (t * SLABS + u), 2 * (t * SLABS + u) + 2):
                 for k in range(3):
-                    send(proj.at[b, (x + k + 1) % 4], xr.at[b, k], sent.at[0], xsem.at[b], x_peers[k])
-
+                    send(proj.at[b, (x + k + 1) % 4], xr.at[b, k], sent, xsem.at[b], x_peers[k])
+
+    pl.semaphore_wait(passed, len(told))
     small[2].wait()
     place_of = lambda r: 16 * (r // PART) + r % PART
     to_slots = (
@@ -235,7 +244,7 @@
             for k in range(8):
                 wt[b, k] = part[16 * k : 16 * k + PART]
             for k in range(7):
-                send(wt.at[b, (me + k + 1) % 8], wr.at[b, k], sent.at[1], rsem.at[b], yc_peers[k])
+                send(wt.at[b, (me + k + 1) % 8], wr.at[b, k], sent, rsem.at[b], yc_peers[k])
         elif kind == 1:
             arrived(wr.at[b], rsem.at[b])
             part = wt[b, me]
@@ -243,7 +252,7 @@
                 part = part + wr[b, k]
             ws[b] = part
             for k in range(7):
-                send(ws.at[b], wz.at[b, k], sent.at[2], zsem.at[b], z_peers[k])
+                send(ws.at[b], wz.at[b, k], sent, zsem.at[b], z_peers[k])
         elif kind == 2:
             arrived(wz.at[b], zsem.at[b])
             part = ws[b]
@@ -252,48 +261,44 @@
             wf[b, me, 0:PART] = part
             mine = wf.at[b, me, pl.ds(0, PART)]
             for k in range(7):
-                send(mine, mine, sent.at[3], asem.at[b], yc_peers[k])
+                send(mine, mine, sent, asem.at[b], yc_peers[k])
         else:
             arrived(wr.at[b], asem.at[b])
             acc = acc + contract_lanes(pz[b], wf[b].reshape(128, 128))
     img[...] = pack_image(contract_lanes(acc, to_slots))
     for k in range(8):
-        send(img, ir.at[k], sent.at[4], isem, i_peers[k])
+        send(img, ir.at[k], sent, isem, i_peers[k])
     arrived(ir, isem)
     image = ir[0]
     for k in range(1, 8):
         image = image + ir[k]
     image = unpack_image(image)
     summed[...] = image
-    back = send(summed, home, sent.at[5], hsem, z_peers[1])
+    send(summed, home, sent, hsem, z_peers[1])
     gp[...] = pack_gram(
         lax.dot_general(image, image, (((0,), (0,)), ((), ())), precision=HIGHEST, preferred_element_type=F32)
     )
     half = RLON // 4
     sibling = device(x, z, y, 1 - core)
     mine, other = (pl.ds(pl.multiple_of(half * c, 8), half) for c in (core, 1 - core))
-    first = send(gp.at[other], gr, sent.at[6], gsem.at[0], sibling)
-    first.wait_recv()
+    send(gp.at[other], gr, sent, gsem.at[0], sibling)
+    arrived(gr, gsem.at[0])
     gh[...] = gp[mine] + gr[...]
     for k in range(15):
-        send(gh, go.at[k], sent.at[7], gsem.at[1], g_peers[k])
+        send(gh, go.at[k], sent, gsem.at[1], g_peers[k])
     arrived(go, gsem.at[1])
     total = gh[...]
     for k in range(15):
         total = total + go[k]
     gf[mine] = total
-    last = send(gf.at[mine], gf.at[mine], sent.at[8], gsem.at[2], sibling)
-    last.wait_recv()
-    back.wait_recv()
+    send(gf.at[mine], gf.at[mine], sent, gsem.at[2], sibling)
+    arrived(gr, gsem.at[2])
+    arrived(home, hsem)
     image_t = jnp.concatenate([home[...].T[0:RLON], jnp.zeros((RLON, 128 - ROWS), F32)], 1)
     solve(total_rows, unpack_gram(gf[...]), image_t, out, yt)
 
-    for k, ref in enumerate((xr, wr, wz, wr, ir)):
-        arrived(ref, sent.at[k])
-    back.wait_send()
-    first.wait_send()
-    arrived(go, sent.at[7])
-    last.wait_send()
+    refs = (xr, wr, wz, wr, ir, home, gr, go, gr)
+    arrived(fv.at[pl.ds(0, sum(math.prod(ref.shape) // 128 for ref in refs))], sent)
 
 
 def body(field, lat_factor, lev_factor, old_factor):
@@ -331,9 +336,10 @@
             pltpu.VMEM((15, RLON // 4, 128), F32),
             pltpu.VMEM((RLON // 2, 128), F32),
             pltpu.VMEM((RLON, 128), F32),
-            dma((TIMES,)),
             dma((3,)),
-            dma((9,)),
+            dma((3,)),
+            pltpu.SemaphoreType.REGULAR,
+            dma,
             dma((BLOCKS,)),
             dma((BLOCKS,)),
             dma((BLOCKS,)),

time: 59.9 us -> 59.2 us (0.988)
  Pallas kernels: 59.1 us -> 58.4 us
    pallas_call x1, Pallas kernels: 59.1 us -> 58.4 us  [body(): pl.pallas_call(functools.partial(hooi_kernel, total_rows), out_shape=pltp...]
where the time goes in v6:
time: 59.2 us; the launch traced here: 59.1 us
  Pallas kernels  58.4 us (99%)
  local copies, waits for them, and re-layouts  0.61 us (1%)
    pallas_call x1, Pallas kernels, body(): pl.pallas_call(functools.partial(hooi_kernel, total_rows), out_shape=pltp...  58.4 us

profile of v6, /device:TPU:1, one launch (start us, length us, event | category | flops | bytes accessed | tf_op | source)
XLA Modules:
  0.0 59.1 jit_solution(10502553609256121259)
XLA Ops:
  0.0 58.4 %shard_map.46 = f32[48,96]{1,0:T(8,128)S(1)} custom-call(f32[9216,128]{1,0:T(8,128)} %bitcast.2, f32[96,96]{1,0:T(8,128)} %lat.1, f32[32,128]{1,0:T(8,128)} %bitcast.3, f32[48,96]{1,0:T(8,128)} %old.1), custom_call_target="tpu_custom_call" | custom-call | tf_op jit(solution)/shard_map/pallas_call | solution.py:309
  58.5 0.6 %copy.6 = f32[48,96]{1,0:T(8,128)} copy(f32[48,96]{1,0:T(8,128)S(1)} %shard_map.46) | data formatting | bytes 36864

commit v7 on v6

--- a/solution.py
+++ b/solution.py
@@ -17,7 +17,10 @@
 BLOCKS = TIMES * SLABS * 2
 LOADS = (0, 16), (16, 32), (48, 48)
 PART = RLON // 8
-SCHEDULE = sorted((b + lag, kind, b) for b in range(BLOCKS) for kind, lag in enumerate((0, 4.6, 11, 16)))
+GROUPS = tuple((b, 1) for b in range(BLOCKS))
+SCHEDULE = sorted(
+    (first + count + lag, kind, g) for g, (first, count) in enumerate(GROUPS) for kind, lag in enumerate((0, 4.6, 11, 16))
+)
 
 
 def split(v):
@@ -25,6 +28,12 @@
     return hi, (v - hi.astype(F32)).astype(BF16)
 
 
+def dot3(a, b, dims):
+    (ah, al), (bh, bl) = a, b
+    dot = functools.partial(lax.dot_general, dimension_numbers=(dims, ((), ())), preferred_element_type=F32)
+    return dot(ah, bh) + (dot(al, bh) + dot(ah, bl))
+
+
 def place():
     lon, lat = lax.axis_index("lon"), lax.axis_index("lat")
     return lat // 2, (lat % 2) * 4 + lon // 8, (lon // 2) % 4, lon % 2
@@ -34,8 +43,13 @@
     return (z % 4) * 8 + y * 2 + core, x * 2 + z // 4
 
 
-def contract_lanes(a, b):
-    return lax.dot_general(a, b, (((1,), (1,)), ((), ())), precision=HIGHEST, preferred_element_type=F32)
+def from_slots(v, to_slots):
+    total = jnp.zeros_like(v)
+    for _ in range(3):
+        piece = v.astype(BF16)
+        v = v - piece.astype(F32)
+        total = total + lax.dot_general(piece, to_slots, (((1,), (1,)), ((), ())), preferred_element_type=F32)
+    return total
 
 
 IMAGE_ROWS = 40
@@ -68,19 +82,22 @@
     return jnp.where(lane <= row, pltpu.roll(low, 128 - half, 1), rest)
 
 
-def unpack_gram(v):
+def unpack_top(v):
+    return jnp.where(lanes_of(v) < RLON // 2, pltpu.roll(v, 127, 1), pltpu.roll(v, 112, 1))
+
+
+def unpack_low(v):
     half = RLON // 2
-    top = jnp.where(lanes_of(v) < half, pltpu.roll(v, 127, 1), pltpu.roll(v, 112, 1))
     square = jnp.concatenate([v, jnp.zeros((128 - half, 128), F32)], 0).T
-    return jnp.concatenate([top, pltpu.roll(square[:half], half, 1)], 0)
+    return pltpu.roll(square[:half], half, 1)
 
 
 PANEL = 16
 
 
-def solve(total_rows, top, image_t, out, yt):
+def solve(total_rows, head, rest, image_t, out, yt):
     tiles = RLON // 8
-    left = [top[8 * r : 8 * r + 8] for r in range(tiles)]
+    left = [head[8 * r : 8 * r + 8] for r in range(PANEL // 8)]
     right = [image_t[8 * r : 8 * r + 8] for r in range(tiles)]
     sub = lax.broadcasted_iota(jnp.int32, (8, 128), 0)
     diagonal = lax.broadcasted_iota(jnp.int32, (8, 128), 1) - sub
@@ -110,6 +127,9 @@
             for p in range(1, 8):
                 rows = jnp.where(sub == p, vr[8 * s + p], rows)
             yt[at + 8 * s : at + 8 * s + 8] = rows
+        if j == 0:
+            top = rest()
+            left += [top[8 * r : 8 * r + 8] for r in range(tiles - PANEL // 8)]
         for r in range(first + PANEL // 8, tiles):
             ml, mr = [], []
             for p in range(PANEL):
@@ -126,7 +146,7 @@
 def hooi_kernel(
     total_rows, field, lat, lev_t, old, out,
     fv, lat_in, lev_in, old_in, lats, lvl, proj, xr, pz, wt, wr, ws, wz, wf, img, ir, summed, home, gp, gr, gh, go, gf,
-    yt, fsem, csem, passed, sent, xsem, rsem, zsem, asem, isem, hsem, gsem,
+    yt, fsem, csem, passed, sent, xsem, rsem, zsem, isem, hsem, gsem,
 ):
     x, z, y, core = place()
     me = y * 2 + core
@@ -221,9 +241,11 @@
                 pl.semaphore_wait(barrier, len(greeted))
                 for peer in told:
                     pl.semaphore_signal(passed, inc=1, device_id=peer, device_id_type=MESH)
-            for b in range(2 * (t * SLABS + u), 2 * (t * SLABS + u) + 2):
-                for k in range(3):
-                    send(proj.at[b, (x + k + 1) % 4], xr.at[b, k], sent, xsem.at[b], x_peers[k])
+            for g, (first, count) in enumerate(GROUPS):
+                if first // 2 == t * SLABS + u:
+                    blocks = pl.ds(first, count)
+                    for k in range(3):
+                        send(proj.at[blocks, (x + k + 1) % 4], xr.at[blocks, k], sent, xsem.at[g], x_peers[k])
 
     pl.semaphore_wait(passed, len(told))
     small[2].wait()
@@ -232,40 +254,48 @@
         place_of(lax.broadcasted_iota(jnp.int32, (128, 128), 0)) == lax.broadcasted_iota(jnp.int32, (128, 128), 1)
     ).astype(F32)
     to_slots = jnp.where(lax.broadcasted_iota(jnp.int32, (128, 128), 0) < RLON, to_slots, 0.0)
-    old_t = jnp.dot(old_in[...], to_slots[:RLON], precision=HIGHEST, preferred_element_type=F32).T
+    old_t = jnp.dot(old_in[...], to_slots[:RLON], precision=HIGHEST, preferred_element_type=F32)
+    old_t = split(old_t.T)
+    to_slots = to_slots.astype(BF16)
     wf[...] = jnp.zeros_like(wf)
     acc = jnp.zeros((ROWS, 128), F32)
 
-    for at, kind, b in SCHEDULE:
+    for at, kind, g in SCHEDULE:
+        first, count = GROUPS[g]
+        blocks = pl.ds(first, count)
         if kind == 0:
-            arrived(xr.at[b], xsem.at[b])
-            pz[b] = proj[b, x] + xr[b, 0] + xr[b, 1] + xr[b, 2]
-            part = jnp.dot(old_t, pz[b], precision=HIGHEST, preferred_element_type=F32)
-            for k in range(8):
-                wt[b, k] = part[16 * k : 16 * k + PART]
+            arrived(xr.at[blocks], xsem.at[g])
+            for b in range(first, first + count):
+                pz[b] = proj[b, x] + xr[b, 0] + xr[b, 1] + xr[b, 2]
+                part = dot3(old_t, split(pz[b]), ((1,), (0,)))
+                for k in range(8):
+                    wt[b, k] = part[16 * k : 16 * k + PART]
             for k in range(7):
-                send(wt.at[b, (me + k + 1) % 8], wr.at[b, k], sent, rsem.at[b], yc_peers[k])
+                send(wt.at[blocks, (me + k + 1) % 8], wr.at[blocks, k], sent, rsem.at[g], yc_peers[k])
         elif kind == 1:
-            arrived(wr.at[b], rsem.at[b])
-            part = wt[b, me]
+            arrived(wr.at[blocks], rsem.at[g])
+            for b in range(first, first + count):
+                part = wt[b, me]
+                for k in range(7):
+                    part = part + wr[b, k]
+                ws[b] = part
             for k in range(7):
-                part = part + wr[b, k]
-            ws[b] = part
+                send(ws.at[blocks], wz.at[blocks, k], sent, zsem.at[g], z_peers[k])
+        elif kind == 2:
+            arrived(wz.at[blocks], zsem.at[g])
+            for b in range(first, first + count):
+                part = ws[b]
+                for k in range(7):
+                    part = part + wz[b, k]
+                wf[b, me, 0:PART] = part
+            mine = wf.at[blocks, me, pl.ds(0, PART)]
             for k in range(7):
-                send(ws.at[b], wz.at[b, k], sent, zsem.at[b], z_peers[k])
-        elif kind == 2:
-            arrived(wz.at[b], zsem.at[b])
-            part = ws[b]
-            for k in range(7):
-                part = part + wz[b, k]
-            wf[b, me, 0:PART] = part
-            mine = wf.at[b, me, pl.ds(0, PART)]
-            for k in range(7):
-                send(mine, mine, sent, asem.at[b], yc_peers[k])
+                send(mine, mine, sent, xsem.at[g], yc_peers[k])
         else:
-            arrived(wr.at[b], asem.at[b])
-            acc = acc + contract_lanes(pz[b], wf[b].reshape(128, 128))
-    img[...] = pack_image(contract_lanes(acc, to_slots))
+            arrived(wr.at[blocks], xsem.at[g])
+            for b in range(first, first + count):
+                acc = acc + dot3(split(pz[b]), split(wf[b].reshape(128, 128)), ((1,), (1,)))
+    img[...] = pack_image(from_slots(acc, to_slots))
     for k in range(8):
         send(img, ir.at[k], sent, isem, i_peers[k])
     arrived(ir, isem)
@@ -280,22 +310,33 @@
     )
     half = RLON // 4
     sibling = device(x, z, y, 1 - core)
-    mine, other = (pl.ds(pl.multiple_of(half * c, 8), half) for c in (core, 1 - core))
+    mine, other = (pl.ds(pl.multiple_of(half * c, 8), half) for c in (1 - core, core))
     send(gp.at[other], gr, sent, gsem.at[0], sibling)
     arrived(gr, gsem.at[0])
     gh[...] = gp[mine] + gr[...]
     for k in range(15):
         send(gh, go.at[k], sent, gsem.at[1], g_peers[k])
+    arrived(home, hsem)
+    image_t = jnp.concatenate([home[...].T[0:RLON], jnp.zeros((RLON, 128 - ROWS), F32)], 1)
     arrived(go, gsem.at[1])
     total = gh[...]
     for k in range(15):
         total = total + go[k]
     gf[mine] = total
     send(gf.at[mine], gf.at[mine], sent, gsem.at[2], sibling)
-    arrived(gr, gsem.at[2])
-    arrived(home, hsem)
-    image_t = jnp.concatenate([home[...].T[0:RLON], jnp.zeros((RLON, 128 - ROWS), F32)], 1)
-    solve(total_rows, unpack_gram(gf[...]), image_t, out, yt)
+
+    @pl.when(core == 0)
+    def _():
+        arrived(gr, gsem.at[2])
+
+    def rest():
+        @pl.when(core == 1)
+        def _():
+            arrived(gr, gsem.at[2])
+
+        return jnp.concatenate([unpack_top(gf[PANEL:]), unpack_low(gf[...])], 0)
+
+    solve(total_rows, unpack_top(gf[0:PANEL]), rest, image_t, out, yt)
 
     refs = (xr, wr, wz, wr, ir, home, gr, go, gr)
     arrived(fv.at[pl.ds(0, sum(math.prod(ref.shape) // 128 for ref in refs))], sent)
@@ -340,10 +381,9 @@
             dma((3,)),
             pltpu.SemaphoreType.REGULAR,
             dma,
-            dma((BLOCKS,)),
-            dma((BLOCKS,)),
-            dma((BLOCKS,)),
-            dma((BLOCKS,)),
+            dma((len(GROUPS),)),
+            dma((len(GROUPS),)),
+            dma((len(GROUPS),)),
             dma,
             dma,
             dma((3,)),

time: 59.2 us -> 58.4 us (0.986)
  Pallas kernels: 58.4 us -> 57.7 us
    pallas_call x1, Pallas kernels: 58.4 us -> 57.7 us  [body(): pl.pallas_call(functools.partial(hooi_kernel, total_rows), out_shape=pltp...]
where the time goes in v7:
time: 58.4 us; the launch traced here: 58.3 us
  Pallas kernels  57.7 us (99%)
  local copies, waits for them, and re-layouts  0.61 us (1%)
    pallas_call x1, Pallas kernels, body(): pl.pallas_call(functools.partial(hooi_kernel, total_rows), out_shape=pltp...  57.7 us

profile of v7, /device:TPU:1, one launch (start us, length us, event | category | flops | bytes accessed | tf_op | source)
XLA Modules:
  0.0 58.3 jit_solution(17640185909477370999)
XLA Ops:
  0.0 57.7 %shard_map.46 = f32[48,96]{1,0:T(8,128)S(1)} custom-call(f32[9216,128]{1,0:T(8,128)} %bitcast.2, f32[96,96]{1,0:T(8,128)} %lat.1, f32[32,128]{1,0:T(8,128)} %bitcast.3, f32[48,96]{1,0:T(8,128)} %old.1), custom_call_target="tpu_custom_call" | custom-call | tf_op jit(solution)/shard_map/pallas_call | solution.py:350
  57.7 0.6 %copy.6 = f32[48,96]{1,0:T(8,128)} copy(f32[48,96]{1,0:T(8,128)S(1)} %shard_map.46) | data formatting | bytes 36864

commit v8 on v7

--- a/solution.py
+++ b/solution.py
@@ -16,6 +16,7 @@
 SLABS = 3
 BLOCKS = TIMES * SLABS * 2
 LOADS = (0, 16), (16, 32), (48, 48)
+FAR_FIRST = (3, 2, 4, 1, 5, 0, 6)
 PART = RLON // 8
 GROUPS = tuple((b, 1) for b in range(BLOCKS))
 SCHEDULE = sorted(
@@ -41,15 +42,6 @@
 
 def device(x, z, y, core):
     return (z % 4) * 8 + y * 2 + core, x * 2 + z // 4
-
-
-def from_slots(v, to_slots):
-    total = jnp.zeros_like(v)
-    for _ in range(3):
-        piece = v.astype(BF16)
-        v = v - piece.astype(F32)
-        total = total + lax.dot_general(piece, to_slots, (((1,), (1,)), ((), ())), preferred_element_type=F32)
-    return total
 
 
 IMAGE_ROWS = 40
@@ -178,8 +170,9 @@
     y_peers = [device(x, z, (y + dy) % 4, core) for dy in (1, 2, 3)]
     z_peers = [device(x, (z + dz) % 8, y, core) for dz in range(1, 8)]
     yc_peers = [device(x, z, ((me + j) % 8) // 2, (me + j) % 2) for j in range(1, 8)]
-    i_peers = [device((x + dx) % 4, (z + dz) % 8, y, core) for dx in range(4) for dz in (2, 6)]
+    i_peers = [device((x + dx) % 4, (z + dz) % 8, y, core) for dx in (2, 1, 3, 0) for dz in (2, 6)]
     g_steps = [(dy, dz) for dy in range(4) for dz in (0, 1, 7, 2 if dy < 2 else 6)][1:]
+    g_steps.sort(key=lambda step: -min(step[0], 4 - step[0]) - min(step[1], 8 - step[1]))
     g_peers = [device(x, (z + dz) % 8, (y + dy) % 4, core) for dy, dz in g_steps]
 
     greeted = x_peers + yc_peers + [z_peers[k] for k in (1, 5, 0, 6)]
@@ -244,21 +237,13 @@
             for g, (first, count) in enumerate(GROUPS):
                 if first // 2 == t * SLABS + u:
                     blocks = pl.ds(first, count)
-                    for k in range(3):
+                    for k in (1, 0, 2):
                         send(proj.at[blocks, (x + k + 1) % 4], xr.at[blocks, k], sent, xsem.at[g], x_peers[k])
 
     pl.semaphore_wait(passed, len(told))
     small[2].wait()
-    place_of = lambda r: 16 * (r // PART) + r % PART
-    to_slots = (
-        place_of(lax.broadcasted_iota(jnp.int32, (128, 128), 0)) == lax.broadcasted_iota(jnp.int32, (128, 128), 1)
-    ).astype(F32)
-    to_slots = jnp.where(lax.broadcasted_iota(jnp.int32, (128, 128), 0) < RLON, to_slots, 0.0)
-    old_t = jnp.dot(old_in[...], to_slots[:RLON], precision=HIGHEST, preferred_element_type=F32)
-    old_t = split(old_t.T)
-    to_slots = to_slots.astype(BF16)
-    wf[...] = jnp.zeros_like(wf)
-    acc = jnp.zeros((ROWS, 128), F32)
+    old_t = split(old_in[...].T)
+    acc = jnp.zeros((ROWS, RLON), F32)
 
     for at, kind, g in SCHEDULE:
         first, count = GROUPS[g]
@@ -267,19 +252,18 @@
             arrived(xr.at[blocks], xsem.at[g])
             for b in range(first, first + count):
                 pz[b] = proj[b, x] + xr[b, 0] + xr[b, 1] + xr[b, 2]
-                part = dot3(old_t, split(pz[b]), ((1,), (0,)))
-                for k in range(8):
-                    wt[b, k] = part[16 * k : 16 * k + PART]
-            for k in range(7):
-                send(wt.at[blocks, (me + k + 1) % 8], wr.at[blocks, k], sent, rsem.at[g], yc_peers[k])
+                wt[b] = dot3(old_t, split(pz[b]), ((1,), (0,)))
+            for k in FAR_FIRST:
+                part = pl.ds(PART * ((me + k + 1) % 8), PART)
+                send(wt.at[blocks, part], wr.at[blocks, k], sent, rsem.at[g], yc_peers[k])
         elif kind == 1:
             arrived(wr.at[blocks], rsem.at[g])
             for b in range(first, first + count):
-                part = wt[b, me]
+                part = wt[b, pl.ds(PART * me, PART)]
                 for k in range(7):
                     part = part + wr[b, k]
                 ws[b] = part
-            for k in range(7):
+            for k in FAR_FIRST:
                 send(ws.at[blocks], wz.at[blocks, k], sent, zsem.at[g], z_peers[k])
         elif kind == 2:
             arrived(wz.at[blocks], zsem.at[g])
@@ -287,15 +271,15 @@
                 part = ws[b]
                 for k in range(7):
                     part = part + wz[b, k]
-                wf[b, me, 0:PART] = part
-            mine = wf.at[blocks, me, pl.ds(0, PART)]
-            for k in range(7):
+                wf[b, pl.ds(PART * me, PART)] = part
+            mine = wf.at[blocks, pl.ds(PART * me, PART)]
+            for k in FAR_FIRST:
                 send(mine, mine, sent, xsem.at[g], yc_peers[k])
         else:
             arrived(wr.at[blocks], xsem.at[g])
             for b in range(first, first + count):
-                acc = acc + dot3(split(pz[b]), split(wf[b].reshape(128, 128)), ((1,), (1,)))
-    img[...] = pack_image(from_slots(acc, to_slots))
+                acc = acc + dot3(split(pz[b]), split(wf[b]), ((1,), (1,)))
+    img[...] = pack_image(jnp.concatenate([acc, jnp.zeros((ROWS, 128 - RLON), F32)], 1))
     for k in range(8):
         send(img, ir.at[k], sent, isem, i_peers[k])
     arrived(ir, isem)
@@ -362,11 +346,11 @@
             pltpu.VMEM((BLOCKS, 4, ROWS, 128), F32),
             pltpu.VMEM((BLOCKS, 3, ROWS, 128), F32),
             pltpu.VMEM((BLOCKS, ROWS, 128), F32),
-            pltpu.VMEM((BLOCKS, 8, PART, 128), F32),
+            pltpu.VMEM((BLOCKS, RLON, 128), F32),
             pltpu.VMEM((BLOCKS, 7, PART, 128), F32),
             pltpu.VMEM((BLOCKS, PART, 128), F32),
             pltpu.VMEM((BLOCKS, 7, PART, 128), F32),
-            pltpu.VMEM((BLOCKS, 8, 16, 128), F32),
+            pltpu.VMEM((BLOCKS, RLON, 128), F32),
             pltpu.VMEM((IMAGE_ROWS, 128), F32),
             pltpu.VMEM((8, IMAGE_ROWS, 128), F32),
             pltpu.VMEM((ROWS, 128), F32),

time: 58.4 us -> 56.2 us (0.962)
  Pallas kernels: 57.7 us -> 55.4 us
    pallas_call x1, Pallas kernels: 57.7 us -> 55.4 us  [body(): pl.pallas_call(functools.partial(hooi_kernel, total_rows), out_shape=pltp...]
where the time goes in v8:
time: 56.2 us; the launch traced here: 56.1 us
  Pallas kernels  55.4 us (99%)
  local copies, waits for them, and re-layouts  0.61 us (1%)
    pallas_call x1, Pallas kernels, body(): pl.pallas_call(functools.partial(hooi_kernel, total_rows), out_shape=pltp...  55.4 us

profile of v8, /device:TPU:1, one launch (start us, length us, event | category | flops | bytes accessed | tf_op | source)
XLA Modules:
  0.0 56.1 jit_solution(12734449322028492495)
XLA Ops:
  0.0 55.4 %shard_map.46 = f32[48,96]{1,0:T(8,128)S(1)} custom-call(f32[9216,128]{1,0:T(8,128)} %bitcast.2, f32[96,96]{1,0:T(8,128)} %lat.1, f32[32,128]{1,0:T(8,128)} %bitcast.3, f32[48,96]{1,0:T(8,128)} %old.1), custom_call_target="tpu_custom_call" | custom-call | tf_op jit(solution)/shard_map/pallas_call | solution.py:334
  55.4 0.6 %copy.6 = f32[48,96]{1,0:T(8,128)} copy(f32[48,96]{1,0:T(8,128)S(1)} %shard_map.46) | data formatting | bytes 36864

commit v9 on v8

--- a/solution.py
+++ b/solution.py
@@ -84,54 +84,63 @@
     return pltpu.roll(square[:half], half, 1)
 
 
-PANEL = 16
+HEAD = 16
+
+
+def tree_sum(terms):
+    while len(terms) > 1:
+        terms = [a + b for a, b in zip(terms[::2], terms[1::2])]
+    return terms[0]
 
 
 def solve(total_rows, head, rest, image_t, out, yt):
     tiles = RLON // 8
-    left = [head[8 * r : 8 * r + 8] for r in range(PANEL // 8)]
+    left = [head[8 * r : 8 * r + 8] for r in range(HEAD // 8)]
     right = [image_t[8 * r : 8 * r + 8] for r in range(tiles)]
     sub = lax.broadcasted_iota(jnp.int32, (8, 128), 0)
     diagonal = lax.broadcasted_iota(jnp.int32, (8, 128), 1) - sub
     spread = lambda v: jnp.broadcast_to(v, (8, 128))
-    for j in range(RLON // PANEL):
-        at, first = PANEL * j, PANEL // 8 * j
-        col = [
-            [spread(left[first + s][:, at + q : at + q + 1]) if q >= 8 * s else None for q in range(PANEL)]
-            for s in range(PANEL // 8)
-        ]
-        d = [[spread(col[p // 8][q][p % 8 : p % 8 + 1]) for p in range(q + 1)] for q in range(PANEL)]
-        vl = [spread(left[first + p // 8][p % 8 : p % 8 + 1]) for p in range(PANEL)]
-        vr = [spread(right[first + p // 8][p % 8 : p % 8 + 1]) for p in range(PANEL)]
-        for p in range(PANEL):
+
+    def down(row, r):
+        return spread(jnp.sum(jnp.where(diagonal == 8 * r, row, 0.0), axis=1, keepdims=True))
+
+    col = [spread(left[0][:, q : q + 1]) for q in range(8)]
+    for j in range(tiles):
+        at = 8 * j
+        d = [[spread(col[q][p : p + 1]) for p in range(q + 1)] for q in range(8)]
+        vl = [spread(left[j][p : p + 1]) for p in range(8)]
+        vr = [spread(right[j][p : p + 1]) for p in range(8)]
+        if j + 1 < tiles:
+            col = [spread(left[j + 1][:, at + 8 + q : at + 9 + q]) for q in range(8)]
+            m = [down(vl[p], j + 1) for p in range(8)]
+        else:
+            m = [jnp.zeros((8, 128), F32)] * 8
+        for p in range(8):
             inv = lax.rsqrt(d[p][p])
-            for q in range(p + 1, PANEL):
+            for q in range(p + 1, 8):
                 d[q][p] = d[q][p] * inv
-            for q in range(p + 1, PANEL):
+            for q in range(p + 1, 8):
                 for r in range(p + 1, q + 1):
                     d[q][r] = d[q][r] - d[q][p] * d[r][p]
-            vl[p], vr[p] = vl[p] * inv, vr[p] * inv
-            for q in range(p + 1, PANEL):
+            vl[p], vr[p], m[p] = vl[p] * inv, vr[p] * inv, m[p] * inv
+            for q in range(p + 1, 8):
                 vl[q] = vl[q] - d[q][p] * vl[p]
                 vr[q] = vr[q] - d[q][p] * vr[p]
-        for s in range(PANEL // 8):
-            rows = vr[8 * s]
-            for p in range(1, 8):
-                rows = jnp.where(sub == p, vr[8 * s + p], rows)
-            yt[at + 8 * s : at + 8 * s + 8] = rows
+                m[q] = m[q] - d[q][p] * m[p]
+        rows = vr[0]
+        for p in range(1, 8):
+            rows = jnp.where(sub == p, vr[p], rows)
+        yt[at : at + 8] = rows
         if j == 0:
-            top = rest()
-            left += [top[8 * r : 8 * r + 8] for r in range(tiles - PANEL // 8)]
-        for r in range(first + PANEL // 8, tiles):
-            ml, mr = [], []
-            for p in range(PANEL):
-                c = jnp.sum(jnp.where(diagonal == 8 * r, vl[p], 0.0), axis=1, keepdims=True)
-                ml.append(c * vl[p])
-                mr.append(c * vr[p])
-            while len(ml) > 1:
-                ml = [a + b for a, b in zip(ml[::2], ml[1::2])]
-                mr = [a + b for a, b in zip(mr[::2], mr[1::2])]
-            left[r], right[r] = left[r] - ml[0], right[r] - mr[0]
+            more = rest()
+            left += [more[8 * r : 8 * r + 8] for r in range(tiles - HEAD // 8)]
+        for r in range(j + 1, tiles):
+            if r == j + 1:
+                col = [col[q] - tree_sum([m[p] * spread(m[p][q : q + 1]) for p in range(8)]) for q in range(8)]
+            else:
+                m = [down(vl[p], r) for p in range(8)]
+            left[r] = left[r] - tree_sum([m[p] * vl[p] for p in range(8)])
+            right[r] = right[r] - tree_sum([m[p] * vr[p] for p in range(8)])
     out[...] = yt[...].T[0:ROWS] * jnp.sqrt(F32(total_rows))
 
 
@@ -167,7 +176,6 @@
         load.start()
 
     x_peers = [device((x + dx) % 4, z, y, core) for dx in (1, 2, 3)]
-    y_peers = [device(x, z, (y + dy) % 4, core) for dy in (1, 2, 3)]
     z_peers = [device(x, (z + dz) % 8, y, core) for dz in range(1, 8)]
     yc_peers = [device(x, z, ((me + j) % 8) // 2, (me + j) % 2) for j in range(1, 8)]
     i_peers = [device((x + dx) % 4, (z + dz) % 8, y, core) for dx in (2, 1, 3, 0) for dz in (2, 6)]
@@ -179,7 +187,7 @@
     barrier = pltpu.get_barrier_semaphore()
     for peer in greeted:
         pl.semaphore_signal(barrier, inc=1, device_id=peer, device_id_type=MESH)
-    told = x_peers + y_peers + [z_peers[1], z_peers[5]]
+    told = [z_peers[1], z_peers[5]]
 
     small[0].wait()
     small[1].wait()
@@ -318,9 +326,9 @@
         def _():
             arrived(gr, gsem.at[2])
 
-        return jnp.concatenate([unpack_top(gf[PANEL:]), unpack_low(gf[...])], 0)
-
-    solve(total_rows, unpack_top(gf[0:PANEL]), rest, image_t, out, yt)
+        return jnp.concatenate([unpack_top(gf[HEAD:]), unpack_low(gf[...])], 0)
+
+    solve(total_rows, unpack_top(gf[0:HEAD]), rest, image_t, out, yt)
 
     refs = (xr, wr, wz, wr, ir, home, gr, go, gr)
     arrived(fv.at[pl.ds(0, sum(math.prod(ref.shape) // 128 for ref in refs))], sent)

time: 56.2 us -> 55.8 us (level)
  no operation moved by 1% of the time
where the time goes in v9:
time: 55.8 us; the launch traced here: 55.7 us
  Pallas kernels  55 us (99%)
  local copies, waits for them, and re-layouts  0.61 us (1%)
    pallas_call x1, Pallas kernels, body(): pl.pallas_call(functools.partial(hooi_kernel, total_rows), out_shape=pltp...  55 us

profile of v9, /device:TPU:1, one launch (start us, length us, event | category | flops | bytes accessed | tf_op | source)
XLA Modules:
  0.0 55.7 jit_solution(4319626330373392423)
XLA Ops:
  0.0 55.0 %shard_map.46 = f32[48,96]{1,0:T(8,128)S(1)} custom-call(f32[9216,128]{1,0:T(8,128)} %bitcast.2, f32[96,96]{1,0:T(8,128)} %lat.1, f32[32,128]{1,0:T(8,128)} %bitcast.3, f32[48,96]{1,0:T(8,128)} %old.1), custom_call_target="tpu_custom_call" | custom-call | tf_op jit(solution)/shard_map/pallas_call | solution.py:342
  55.1 0.6 %copy.6 = f32[48,96]{1,0:T(8,128)} copy(f32[48,96]{1,0:T(8,128)S(1)} %shard_map.46) | data formatting | bytes 36864

commit v10 on v9

--- a/solution.py
+++ b/solution.py
@@ -15,7 +15,7 @@
 RLAT, RLEV, RLON = 96, 32, 96
 SLABS = 3
 BLOCKS = TIMES * SLABS * 2
-LOADS = (0, 16), (16, 32), (48, 48)
+LOADS = (0, 24), (24, 24), (48, 48)
 FAR_FIRST = (3, 2, 4, 1, 5, 0, 6)
 PART = RLON // 8
 GROUPS = tuple((b, 1) for b in range(BLOCKS))
@@ -44,7 +44,7 @@
     return (z % 4) * 8 + y * 2 + core, x * 2 + z // 4
 
 
-IMAGE_ROWS = 40
+IMAGE_ROWS = 36
 
 
 def lanes_of(v):
@@ -53,15 +53,14 @@
 
 def pack_image(v):
     last = v[IMAGE_ROWS:]
-    tail = [pltpu.roll(last, 96 - 32 * k, 1) for k in range(3)]
-    tail = jnp.concatenate(tail + [jnp.zeros((IMAGE_ROWS - 24, 128), F32)], 0)
+    tail = jnp.concatenate([pltpu.roll(last, 96 - 32 * k, 1) for k in range(3)], 0)
     return jnp.where(lanes_of(tail) < RLON, v[:IMAGE_ROWS], tail)
 
 
 def unpack_image(v):
-    last = jnp.zeros((8, 128), F32)
+    last = jnp.zeros((12, 128), F32)
     for k in range(3):
-        piece = pltpu.roll(v[8 * k : 8 * k + 8], 32 + 32 * k, 1)
+        piece = pltpu.roll(v[12 * k : 12 * k + 12], 32 + 32 * k, 1)
         last = jnp.where(lanes_of(last) // 32 == k, piece, last)
     return jnp.concatenate([jnp.where(lanes_of(v) < RLON, v, 0.0), last], 0)
 
@@ -183,7 +182,8 @@
     g_steps.sort(key=lambda step: -min(step[0], 4 - step[0]) - min(step[1], 8 - step[1]))
     g_peers = [device(x, (z + dz) % 8, (y + dy) % 4, core) for dy, dz in g_steps]
 
-    greeted = x_peers + yc_peers + [z_peers[k] for k in (1, 5, 0, 6)]
+    greeted = [x_peers[1], z_peers[1], z_peers[5]] + [yc_peers[k] for k in FAR_FIRST]
+    greeted += [x_peers[0], x_peers[2], z_peers[0], z_peers[6]]
     barrier = pltpu.get_barrier_semaphore()
     for peer in greeted:
         pl.semaphore_signal(barrier, inc=1, device_id=peer, device_id_type=MESH)
@@ -218,7 +218,7 @@
 
         loads[k].wait()
         at, rows = LOADS[k]
-        lax.fori_loop(at, at + rows, one, 0, unroll=16)
+        lax.fori_loop(at, at + rows, one, 0, unroll=24)
 
     def latitudes(t, u):
         parts = [

time: 55.8 us -> 55 us (0.986)
  Pallas kernels: 55 us -> 54.2 us
    pallas_call x1, Pallas kernels: 55 us -> 54.2 us  [body(): pl.pallas_call(functools.partial(hooi_kernel, total_rows), out_shape=pltp...]
where the time goes in v10:
time: 55 us; the launch traced here: 54.8 us
  Pallas kernels  54.2 us (99%)
  local copies, waits for them, and re-layouts  0.61 us (1%)
    pallas_call x1, Pallas kernels, body(): pl.pallas_call(functools.partial(hooi_kernel, total_rows), out_shape=pltp...  54.2 us

profile of v10, /device:TPU:1, one launch (start us, length us, event | category | flops | bytes accessed | tf_op | source)
XLA Modules:
  0.0 54.8 jit_solution(594075963180208923)
XLA Ops:
  0.0 54.2 %shard_map.46 = f32[48,96]{1,0:T(8,128)S(1)} custom-call(f32[9216,128]{1,0:T(8,128)} %bitcast.2, f32[96,96]{1,0:T(8,128)} %lat.1, f32[32,128]{1,0:T(8,128)} %bitcast.3, f32[48,96]{1,0:T(8,128)} %old.1), custom_call_target="tpu_custom_call" | custom-call | tf_op jit(solution)/shard_map/pallas_call | solution.py:342
  54.2 0.6 %copy.6 = f32[48,96]{1,0:T(8,128)} copy(f32[48,96]{1,0:T(8,128)S(1)} %shard_map.46) | data formatting | bytes 36864

commit v11 on v10

--- a/solution.py
+++ b/solution.py
@@ -83,18 +83,19 @@
     return pltpu.roll(square[:half], half, 1)
 
 
-HEAD = 16
+HEAD = 24
 
 
 def tree_sum(terms):
     while len(terms) > 1:
-        terms = [a + b for a, b in zip(terms[::2], terms[1::2])]
+        terms = [a + b for a, b in zip(terms[::2], terms[1::2])] + terms[len(terms) // 2 * 2 :]
     return terms[0]
 
 
 def solve(total_rows, head, rest, image_t, out, yt):
     tiles = RLON // 8
-    left = [head[8 * r : 8 * r + 8] for r in range(HEAD // 8)]
+    known = HEAD // 8
+    left = [head[8 * r : 8 * r + 8] for r in range(known)]
     right = [image_t[8 * r : 8 * r + 8] for r in range(tiles)]
     sub = lax.broadcasted_iota(jnp.int32, (8, 128), 0)
     diagonal = lax.broadcasted_iota(jnp.int32, (8, 128), 1) - sub
@@ -103,13 +104,14 @@
     def down(row, r):
         return spread(jnp.sum(jnp.where(diagonal == 8 * r, row, 0.0), axis=1, keepdims=True))
 
+    done = []
     col = [spread(left[0][:, q : q + 1]) for q in range(8)]
     for j in range(tiles):
         at = 8 * j
         d = [[spread(col[q][p : p + 1]) for p in range(q + 1)] for q in range(8)]
         vl = [spread(left[j][p : p + 1]) for p in range(8)]
         vr = [spread(right[j][p : p + 1]) for p in range(8)]
-        if j + 1 < tiles:
+        if j + 1 < len(left):
             col = [spread(left[j + 1][:, at + 8 + q : at + 9 + q]) for q in range(8)]
             m = [down(vl[p], j + 1) for p in range(8)]
         else:
@@ -130,10 +132,19 @@
         for p in range(1, 8):
             rows = jnp.where(sub == p, vr[p], rows)
         yt[at : at + 8] = rows
-        if j == 0:
+        done.append((vl, vr))
+        if j == known - 1:
+            late = []
+            for r in range(known, tiles):
+                terms = [(down(row, r), row, y) for rows in done for row, y in zip(*rows)]
+                late.append([tree_sum([t[0] * t[k] for t in terms]) for k in (1, 2)])
             more = rest()
-            left += [more[8 * r : 8 * r + 8] for r in range(tiles - HEAD // 8)]
-        for r in range(j + 1, tiles):
+            for r in range(known, tiles):
+                left.append(more[8 * (r - known) : 8 * (r - known) + 8] - late[r - known][0])
+                right[r] = right[r] - late[r - known][1]
+            col = [spread(left[known][:, HEAD + q : HEAD + q + 1]) for q in range(8)]
+            continue
+        for r in range(j + 1, len(left)):
             if r == j + 1:
                 col = [col[q] - tree_sum([m[p] * spread(m[p][q : q + 1]) for p in range(8)]) for q in range(8)]
             else:

time: 55 us -> 54.4 us (0.989)
  no operation moved by 1% of the time
where the time goes in v11:
time: 54.4 us; the launch traced here: 54.3 us
  Pallas kernels  53.7 us (99%)
  local copies, waits for them, and re-layouts  0.61 us (1%)
    pallas_call x1, Pallas kernels, body(): pl.pallas_call(functools.partial(hooi_kernel, total_rows), out_shape=pltp...  53.7 us

profile of v11, /device:TPU:1, one launch (start us, length us, event | category | flops | bytes accessed | tf_op | source)
XLA Modules:
  0.0 54.3 jit_solution(3541104781275278884)
XLA Ops:
  0.0 53.7 %shard_map.46 = f32[48,96]{1,0:T(8,128)S(1)} custom-call(f32[9216,128]{1,0:T(8,128)} %bitcast.2, f32[96,96]{1,0:T(8,128)} %lat.1, f32[32,128]{1,0:T(8,128)} %bitcast.3, f32[48,96]{1,0:T(8,128)} %old.1), custom_call_target="tpu_custom_call" | custom-call | tf_op jit(solution)/shard_map/pallas_call | solution.py:353
  53.7 0.6 %copy.6 = f32[48,96]{1,0:T(8,128)} copy(f32[48,96]{1,0:T(8,128)S(1)} %shard_map.46) | data formatting | bytes 36864

commit v12 on v11

--- a/solution.py
+++ b/solution.py
@@ -185,13 +185,14 @@
     for load in small + loads:
         load.start()
 
-    x_peers = [device((x + dx) % 4, z, y, core) for dx in (1, 2, 3)]
-    z_peers = [device(x, (z + dz) % 8, y, core) for dz in range(1, 8)]
+    way = 1 + 6 * core
+    x_peers = [device((x + way * dx) % 4, z, y, core) for dx in (1, 2, 3)]
+    z_peers = [device(x, (z + way * dz) % 8, y, core) for dz in range(1, 8)]
     yc_peers = [device(x, z, ((me + j) % 8) // 2, (me + j) % 2) for j in range(1, 8)]
-    i_peers = [device((x + dx) % 4, (z + dz) % 8, y, core) for dx in (2, 1, 3, 0) for dz in (2, 6)]
+    i_peers = [device((x + way * dx) % 4, (z + way * dz) % 8, y, core) for dx in (2, 1, 3, 0) for dz in (2, 6)]
     g_steps = [(dy, dz) for dy in range(4) for dz in (0, 1, 7, 2 if dy < 2 else 6)][1:]
     g_steps.sort(key=lambda step: -min(step[0], 4 - step[0]) - min(step[1], 8 - step[1]))
-    g_peers = [device(x, (z + dz) % 8, (y + dy) % 4, core) for dy, dz in g_steps]
+    g_peers = [device(x, (z + way * dz) % 8, (y + way * dy) % 4, core) for dy, dz in g_steps]
 
     greeted = [x_peers[1], z_peers[1], z_peers[5]] + [yc_peers[k] for k in FAR_FIRST]
     greeted += [x_peers[0], x_peers[2], z_peers[0], z_peers[6]]
@@ -257,7 +258,7 @@
                 if first // 2 == t * SLABS + u:
                     blocks = pl.ds(first, count)
                     for k in (1, 0, 2):
-                        send(proj.at[blocks, (x + k + 1) % 4], xr.at[blocks, k], sent, xsem.at[g], x_peers[k])
+                        send(proj.at[blocks, (x + way * (k + 1)) % 4], xr.at[blocks, k], sent, xsem.at[g], x_peers[k])
 
     pl.semaphore_wait(passed, len(told))
     small[2].wait()

time: 54.4 us -> 54.6 us (level)
  no operation moved by 1% of the time
where the time goes in v12:
time: 54.6 us; the launch traced here: 54.5 us
  Pallas kernels  53.9 us (99%)
  local copies, waits for them, and re-layouts  0.61 us (1%)
    pallas_call x1, Pallas kernels, body(): pl.pallas_call(functools.partial(hooi_kernel, total_rows), out_shape=pltp...  53.9 us

profile of v12, /device:TPU:1, one launch (start us, length us, event | category | flops | bytes accessed | tf_op | source)
XLA Modules:
  0.0 54.5 jit_solution(8424168459811882160)
XLA Ops:
  0.0 53.9 %shard_map.46 = f32[48,96]{1,0:T(8,128)S(1)} custom-call(f32[9216,128]{1,0:T(8,128)} %bitcast.2, f32[96,96]{1,0:T(8,128)} %lat.1, f32[32,128]{1,0:T(8,128)} %bitcast.3, f32[48,96]{1,0:T(8,128)} %old.1), custom_call_target="tpu_custom_call" | custom-call | tf_op jit(solution)/shard_map/pallas_call | solution.py:354
  53.9 0.6 %copy.6 = f32[48,96]{1,0:T(8,128)} copy(f32[48,96]{1,0:T(8,128)S(1)} %shard_map.46) | data formatting | bytes 36864

commit v13 on v11

--- a/solution.py
+++ b/solution.py
@@ -187,13 +187,15 @@
 
     x_peers = [device((x + dx) % 4, z, y, core) for dx in (1, 2, 3)]
     z_peers = [device(x, (z + dz) % 8, y, core) for dz in range(1, 8)]
-    yc_peers = [device(x, z, ((me + j) % 8) // 2, (me + j) % 2) for j in range(1, 8)]
+    yc_steps = [(2, 0), (2, 1), (1, 0), (1, 1), (3, 0), (3, 1), (0, 1)]
+    yc_peers = [device(x, z, (y + dy) % 4, (core + dc) % 2) for dy, dc in yc_steps]
+    yc_parts = [PART * ((y + dy) % 4 * 2 + (core + dc) % 2) for dy, dc in yc_steps]
     i_peers = [device((x + dx) % 4, (z + dz) % 8, y, core) for dx in (2, 1, 3, 0) for dz in (2, 6)]
     g_steps = [(dy, dz) for dy in range(4) for dz in (0, 1, 7, 2 if dy < 2 else 6)][1:]
     g_steps.sort(key=lambda step: -min(step[0], 4 - step[0]) - min(step[1], 8 - step[1]))
     g_peers = [device(x, (z + dz) % 8, (y + dy) % 4, core) for dy, dz in g_steps]
 
-    greeted = [x_peers[1], z_peers[1], z_peers[5]] + [yc_peers[k] for k in FAR_FIRST]
+    greeted = [x_peers[1], z_peers[1], z_peers[5]] + yc_peers
     greeted += [x_peers[0], x_peers[2], z_peers[0], z_peers[6]]
     barrier = pltpu.get_barrier_semaphore()
     for peer in greeted:
@@ -272,8 +274,8 @@
             for b in range(first, first + count):
                 pz[b] = proj[b, x] + xr[b, 0] + xr[b, 1] + xr[b, 2]
                 wt[b] = dot3(old_t, split(pz[b]), ((1,), (0,)))
-            for k in FAR_FIRST:
-                part = pl.ds(PART * ((me + k + 1) % 8), PART)
+            for k in range(7):
+                part = pl.ds(yc_parts[k], PART)
                 send(wt.at[blocks, part], wr.at[blocks, k], sent, rsem.at[g], yc_peers[k])
         elif kind == 1:
             arrived(wr.at[blocks], rsem.at[g])
@@ -292,7 +294,7 @@
                     part = part + wz[b, k]
                 wf[b, pl.ds(PART * me, PART)] = part
             mine = wf.at[blocks, pl.ds(PART * me, PART)]
-            for k in FAR_FIRST:
+            for k in range(7):
                 send(mine, mine, sent, xsem.at[g], yc_peers[k])
         else:
             arrived(wr.at[blocks], xsem.at[g])

time: 54.4 us -> 54.6 us (level)
  no operation moved by 1% of the time
where the time goes in v13:
time: 54.6 us; the launch traced here: 54.4 us
  Pallas kernels  53.8 us (99%)
  local copies, waits for them, and re-layouts  0.61 us (1%)
    pallas_call x1, Pallas kernels, body(): pl.pallas_call(functools.partial(hooi_kernel, total_rows), out_shape=pltp...  53.8 us

profile of v13, /device:TPU:1, one launch (start us, length us, event | category | flops | bytes accessed | tf_op | source)
XLA Modules:
  0.0 54.4 jit_solution(3090225164250384957)
XLA Ops:
  0.0 53.8 %shard_map.46 = f32[48,96]{1,0:T(8,128)S(1)} custom-call(f32[9216,128]{1,0:T(8,128)} %bitcast.2, f32[96,96]{1,0:T(8,128)} %lat.1, f32[32,128]{1,0:T(8,128)} %bitcast.3, f32[48,96]{1,0:T(8,128)} %old.1), custom_call_target="tpu_custom_call" | custom-call | tf_op jit(solution)/shard_map/pallas_call | solution.py:355
  53.8 0.6 %copy.6 = f32[48,96]{1,0:T(8,128)} copy(f32[48,96]{1,0:T(8,128)S(1)} %shard_map.46) | data formatting | bytes 36864

commit v14 on v13

--- a/solution.py
+++ b/solution.py
@@ -280,19 +280,13 @@
         elif kind == 1:
             arrived(wr.at[blocks], rsem.at[g])
             for b in range(first, first + count):
-                part = wt[b, pl.ds(PART * me, PART)]
-                for k in range(7):
-                    part = part + wr[b, k]
-                ws[b] = part
+                ws[b] = tree_sum([wr[b, k] for k in range(7)] + [wt[b, pl.ds(PART * me, PART)]])
             for k in FAR_FIRST:
                 send(ws.at[blocks], wz.at[blocks, k], sent, zsem.at[g], z_peers[k])
         elif kind == 2:
             arrived(wz.at[blocks], zsem.at[g])
             for b in range(first, first + count):
-                part = ws[b]
-                for k in range(7):
-                    part = part + wz[b, k]
-                wf[b, pl.ds(PART * me, PART)] = part
+                wf[b, pl.ds(PART * me, PART)] = tree_sum([wz[b, k] for k in range(7)] + [ws[b]])
             mine = wf.at[blocks, pl.ds(PART * me, PART)]
             for k in range(7):
                 send(mine, mine, sent, xsem.at[g], yc_peers[k])
@@ -304,9 +298,7 @@
     for k in range(8):
         send(img, ir.at[k], sent, isem, i_peers[k])
     arrived(ir, isem)
-    image = ir[0]
-    for k in range(1, 8):
-        image = image + ir[k]
+    image = tree_sum([ir[k] for k in range(8)])
     image = unpack_image(image)
     summed[...] = image
     send(summed, home, sent, hsem, z_peers[1])
@@ -324,10 +316,7 @@
     arrived(home, hsem)
     image_t = jnp.concatenate([home[...].T[0:RLON], jnp.zeros((RLON, 128 - ROWS), F32)], 1)
     arrived(go, gsem.at[1])
-    total = gh[...]
-    for k in range(15):
-        total = total + go[k]
-    gf[mine] = total
+    gf[mine] = tree_sum([go[k] for k in range(15)] + [gh[...]])
     send(gf.at[mine], gf.at[mine], sent, gsem.at[2], sibling)
 
     @pl.when(core == 0)

time: 54.6 us -> 54.6 us (level)
  no operation moved by 1% of the time
where the time goes in v14:
time: 54.6 us; the launch traced here: 54.5 us
  Pallas kernels  53.9 us (99%)
  local copies, waits for them, and re-layouts  0.61 us (1%)
    pallas_call x1, Pallas kernels, body(): pl.pallas_call(functools.partial(hooi_kernel, total_rows), out_shape=pltp...  53.9 us

profile of v14, /device:TPU:1, one launch (start us, length us, event | category | flops | bytes accessed | tf_op | source)
XLA Modules:
  0.0 54.5 jit_solution(6991208836842084549)
XLA Ops:
  0.0 53.9 %shard_map.46 = f32[48,96]{1,0:T(8,128)S(1)} custom-call(f32[9216,128]{1,0:T(8,128)} %bitcast.2, f32[96,96]{1,0:T(8,128)} %lat.1, f32[32,128]{1,0:T(8,128)} %bitcast.3, f32[48,96]{1,0:T(8,128)} %old.1), custom_call_target="tpu_custom_call" | custom-call | tf_op jit(solution)/shard_map/pallas_call | solution.py:344
  53.9 0.6 %copy.6 = f32[48,96]{1,0:T(8,128)} copy(f32[48,96]{1,0:T(8,128)S(1)} %shard_map.46) | data formatting | bytes 36864
